TPU v7x, 256 devices: a whole 4x4x8 slice. The times are simulated.
256 devices in a mesh: section: 8 (over x, y_lo), dp: 32 (over z, y_hi, core).
Axes of the slice: x: 4, y: 4 (y_hi: 2, y_lo: 2; y = y_hi * 2 + y_lo), z: 8, core: 2. Of those that a mesh axis runs over, the one named last changes fastest.
Arguments:
- params: bfloat16 [8, 2560, 2048], P('section', 'dp'), may hold values from -2 to 2
- moment_one: float32 [8, 2560, 2048], P('section', 'dp'), may hold values from -3 to 3
- moment_two: float32 [8, 2560, 2048], P('section', 'dp'), may hold values from 0.05 to 1
- sent_rows: bfloat16 [8, 32, 4, 192, 2048], P('section', 'dp'), may hold values from -6 to 6
- back_rows: bfloat16 [8, 32, 4, 192, 2048], P('section', 'dp'), may hold values from -6 to 6
- slot_ids: int32 [8, 32, 2], P('section', 'dp'), may hold values from 0 to 3, all different within a row
Outputs:
- new_params: bfloat16 [8, 2560, 2048], P('section', 'dp')
- new_moment_one: float32 [8, 2560, 2048], P('section', 'dp')
- new_moment_two: float32 [8, 2560, 2048], P('section', 'dp')
Inputs may be any that keep to these rules, and one draw needn't show every extreme that they name: Each row of slot_ids names 2 different slots.
All inputs are finite; a program needn't handle non-finite values.
Results may differ from a plain program's by a relative error of at most 0.017.
Values may be sent and summed in bfloat16 or wider, within the bound.
A program may use at most 128 MiB of HBM per device.

v0:
```python
import jax
import jax.numpy as jnp
from jax import lax
from jax.sharding import PartitionSpec as P

HEAD_SIZE = 64
QUERY_HEADS = 16
KEY_VALUE_HEADS = 4
STEP = 100


rope_base = 500000.0
learn_rate = 0.0003
decay_rate = 0.1


def shifted(value, axis, steps):
    count = lax.axis_size(axis)
    pairs = [(source, (source + steps) % count) for source in range(count)]
    return lax.ppermute(value, axis, pairs)


def rotary(values, cosine, sine):
    midway = values.shape[-1] // 2
    leading = values[..., :midway]
    trailing = values[..., midway:]
    return jnp.concatenate(
        [leading * cosine - trailing * sine, trailing * cosine + leading * sine], axis=-1
    )


def attention_branch(weights, logged):
    batch_list, sequence_length, width = logged.shape
    tokens = batch_list * sequence_length
    query_total_width = QUERY_HEADS * HEAD_SIZE
    key_value_width = KEY_VALUE_HEADS * HEAD_SIZE
    head_groups = QUERY_HEADS // KEY_VALUE_HEADS
    flat = logged.reshape(tokens, width).astype(jnp.float32)
    scaling = lax.rsqrt(jnp.mean(flat * flat, axis=-1, keepdims=True) + 1e-05)
    normed = (flat * scaling).astype(jnp.bfloat16)
    projected_rows = lax.dot_general(
        normed,
        weights[: query_total_width + 2 * key_value_width],
        (((1,), (1,)), ((), ())),
        preferred_element_type=jnp.float32,
    )
    query_rows = projected_rows[:, :query_total_width].reshape(
        batch_list, sequence_length, KEY_VALUE_HEADS, head_groups, HEAD_SIZE
    )
    key_portion = projected_rows[
        :, query_total_width : query_total_width + key_value_width
    ].reshape(batch_list, sequence_length, KEY_VALUE_HEADS, HEAD_SIZE)
    value_portion = projected_rows[:, query_total_width + key_value_width :].reshape(
        batch_list, sequence_length, KEY_VALUE_HEADS, HEAD_SIZE
    )
    frequency = rope_base ** (-jnp.arange(HEAD_SIZE // 2, dtype=jnp.float32) * 2.0 / HEAD_SIZE)
    angles = jnp.arange(sequence_length, dtype=jnp.float32)[:, None] * frequency[None, :]
    cosine = jnp.cos(angles)
    sine = jnp.sin(angles)
    query_rows = rotary(query_rows, cosine[None, :, None, None, :], sine[None, :, None, None, :])
    key_portion = rotary(key_portion, cosine[None, :, None, :], sine[None, :, None, :])
    scores = jnp.einsum("bqhgd,bkhd->bhgqk", query_rows, key_portion) * HEAD_SIZE ** (-0.5)
    causal = jnp.arange(sequence_length)[:, None] >= jnp.arange(sequence_length)[None, :]
    scores = jnp.where(causal, scores, -1e30)
    highest = lax.stop_gradient(jnp.max(scores, axis=-1, keepdims=True))
    raised = jnp.exp(scores - highest)
    probs = raised / jnp.sum(raised, axis=-1, keepdims=True)
    context = (
        jnp.einsum("bhgqk,bkhd->bqhgd", probs, value_portion)
        .reshape(tokens, query_total_width)
        .astype(jnp.bfloat16)
    )
    return jnp.dot(
        context,
        weights[query_total_width + 2 * key_value_width :],
        preferred_element_type=jnp.float32,
    )


def replay_gradient(weights, logged, upstream):
    batch_list, sequence_length, width = logged.shape
    outcome, pullback = jax.vjp(lambda current: attention_branch(current, logged), weights)
    return pullback(upstream.reshape(batch_list * sequence_length, width).astype(jnp.float32))[0]


def apply_adam(weights, first_moment, second_moment, gradient):
    first_new = 0.9 * first_moment + 0.1 * gradient
    second_new = 0.999 * second_moment + 0.001 * gradient * gradient
    fix_first = 1.0 - 0.9**STEP
    fix_second = 1.0 - 0.999**STEP
    update = first_new / fix_first / (jnp.sqrt(second_new / fix_second) + 1e-08)
    current = weights.astype(jnp.float32)
    renewed = (current - learn_rate * (update + decay_rate * current)).astype(jnp.bfloat16)
    return (renewed, first_new, second_new)


def shards(params, moment_one, moment_two, sent_rows, back_rows, slot_ids):
    gathered = lax.all_gather(params, "dp", axis=1, tiled=True)
    inputs_whole = shifted(sent_rows, "section", 1)
    grads_whole = shifted(back_rows, "section", -1)
    logged = jnp.take(inputs_whole[0, 0], slot_ids[0, 0], axis=0)
    upstream = jnp.take(grads_whole[0, 0], slot_ids[0, 0], axis=0)
    local_grad = replay_gradient(gathered[0], logged, upstream)
    summed = lax.psum_scatter(local_grad, "dp", scatter_dimension=0, tiled=True).astype(jnp.float32)
    renewed, first_new, second_new = apply_adam(
        params[0], moment_one[0], moment_two[0], summed / lax.axis_size("dp")
    )
    return (renewed[None], first_new[None], second_new[None])


def solution(mesh):
    in_specs = (
        P("section", "dp", None),
        P("section", "dp", None),
        P("section", "dp", None),
        P("section", "dp", None, None, None),
        P("section", "dp", None, None, None),
        P("section", "dp", None),
    )
    out_specs = (P("section", "dp", None), P("section", "dp", None), P("section", "dp", None))
    return jax.shard_map(shards, mesh=mesh, in_specs=in_specs, out_specs=out_specs, check_vma=False)
```

profile of v0, /device:TPU:6, one launch (start us, length us, event | category | flops | bytes accessed | tf_op | source)
XLA Modules:
  0.0 464.2 jit_solution(8092474262601134236)
XLA Ops:
  7.9 1.7 collective-permute-start
  9.6 1.3 collective-permute-start.1
  13.2 162.3 %collective-permute-done = bf16[1,1,4,192,2048]{4,3,2,1,0:T(8,128)(2,1)S(1)} collective-permute-done((bf16[1,1,4,192,2048]{4,3,2,1,0:T(8,128)(2,1)}, bf16[1,1,4,192,2048]{4,3,2,1,0:T(8,128)(2,1)S(1)}, u32[]{:S(2)}, u32[]{:S(2)}) %collective-permute-start) | collective-permute-done | bytes 3145760 | tf_op jit(solution)/shard_map/ppermute | solution.py:20
  175.4 1.6 copy-done.7
  177.0 2.5 gather_fusion
  180.2 2.7 gather_fusion.1
  182.9 1.6 multiply_convert_fusion
  184.5 1.5 broadcast_select_fusion
  186.0 1.4 fusion.9
  187.4 19.8 %all-gather.2.cloned.1.call-done = bf16[1,2560,2048]{2,1,0:T(8,128)(2,1)} async-done(((bf16[1,80,2048]{2,1,0:T(8,128)(2,1)}), bf16[1,2560,2048]{2,1,0:T(8,128)(2,1)}) %all-gather.2.cloned.1.call-update) | async-done | bytes 10485776 | tf_op jit(solution)/shard_map/all_gather | solution.py:98
  207.2 5.0 %fusion = f32[384,1536]{1,0:T(8,128)S(1)} fusion(bf16[384,2048]{1,0:T(8,128)(2,1)S(1)} %bitcast.121, bf16[1,2560,2048]{2,1,0:T(8,128)(2,1)} %all-gather.2.cloned.1.call-done), kind=kOutput, calls=%fused_computation.5 | convolution fusion | flops 2415919104 | bytes 10223616 | tf_op jit(solution)/shard_map/jvp()/dot_general | solution.py:41
  216.8 3.4 reshape.207
  220.2 4.8 %fusion.46 = (f32[2,192,4,4,32]{4,3,2,1,0:T(4,128)}, f32[2,192,4,4,32]{4,3,2,1,0:T(4,128)}) fusion(f32[2,192,4,4,64]{4,3,2,1,0:T(4,128)S(1)} %reshape.207), kind=kLoop, calls=%fused_computation.90 | loop fusion | bytes 3145728 | tf_op jit(solution)/shard_map/jvp()/slice | solution.py:26
  224.9 4.5 copy.54
  229.4 2.5 copy.53
  231.9 4.5 fusion.17
  237.6 3.6 reshape.173
  243.9 1.5 fusion.8
  245.5 1.7 convolution_bitcast_fusion.1
  247.2 2.7 fusion.18
  249.9 2.4 multiply_reduce_fusion
  252.4 2.8 fusion.4
  255.2 1.9 fusion.19
  259.3 2.3 copy.27
  261.6 1.4 convert_element_type.57
  263.1 6.0 %convolution_convert_fusion.1 = bf16[1024,2048]{1,0:T(8,128)(2,1)} fusion(bf16[384,1024]{0,1:T(8,128)(2,1)} %convert_element_type.57, bf16[384,2048]{1,0:T(8,128)(2,1)} %bitcast.123), kind=kOutput, calls=%fused_computation.17 | convolution fusion | flops 1612709888 | bytes 6553600 | tf_op jit(solution)/shard_map/transpose(jvp())/dot_general | solution.py:73
  271.8 1.6 copy.35
  273.5 2.8 reshape.176
  276.3 5.7 %convolution_convert_fusion = bf16[1536,2048]{1,0:T(8,128)(2,1)S(1)} fusion(bf16[384,2048]{1,0:T(8,128)(2,1)} %fusion.9, f32[384,1024]{0,1:T(8,128)} %reshape.176, f32[384,256]{0,1:T(8,128)S(1)} %reshape.175, f32[384,256]{0,1:T(8,128)S(1)} %copy-done.11), kind=kOutput, calls=%fused_computation.3 | convolution fusion | flops 2420244480 | bytes 10223616 | tf_op jit(solution)/shard_map/transpose(jvp())/dot_general | solution.py:41
  282.0 12.3 %pad_add_fusion = bf16[2560,2048]{1,0:T(8,128)(2,1)} fusion(bf16[1536,2048]{1,0:T(8,128)(2,1)S(1)} %convolution_convert_fusion, bf16[1024,2048]{1,0:T(8,128)(2,1)S(1)} %copy-done.1), kind=kLoop, calls=%fused_computation.2 | loop fusion | flops 20971520 | bytes 20971520 | tf_op jit(solution)/shard_map/transpose(jvp())/add_any | solution.py:43
  294.4 160.1 %reduce-scatter.2.cloned.1.call-done = bf16[80,2048]{1,0:T(8,128)(2,1)} async-done(((bf16[2560,2048]{1,0:T(8,128)(2,1)}), bf16[80,2048]{1,0:T(8,128)(2,1)}) %reduce-scatter.2.cloned.1.call-update) | async-done | bytes 327696 | tf_op jit(solution)/shard_map/reduce_scatter | solution.py:104
  454.5 2.7 fusion.34
  (64 shorter events, 17.0 us)
Async XLA Ops:
  7.2 200.0 %all-gather.2.cloned.1.call-start = ((), (), s32[]{:S(2)}) async-start(), calls=%async_computation.1 | async-start | bytes 10813440 | tf_op jit(solution)/shard_map/all_gather | solution.py:98
  7.9 446.6 %reduce-scatter.2.cloned.1.call-start = ((), (), s32[]{:S(2)}) async-start(), calls=%async_computation.2 | async-start | bytes 10813440 | tf_op jit(solution)/shard_map/reduce_scatter | solution.py:104
  7.9 167.5 %collective-permute-start = (bf16[1,1,4,192,2048]{4,3,2,1,0:T(8,128)(2,1)}, bf16[1,1,4,192,2048]{4,3,2,1,0:T(8,128)(2,1)S(1)}, u32[]{:S(2)}, u32[]{:S(2)}) collective-permute-start(bf16[1,1,4,192,2048]{4,3,2,1,0:T(8,128)(2,1)} %param.11), channel_id=1, source_target_pairs={{0,32},{32,64},{64,96},{96,128},{128,160},{160,192},{192,224},{224... | collective-permute-start | bytes 9437192 | tf_op jit(solution)/shard_map/ppermute | solution.py:20
  9.6 170.6 %collective-permute-start.1 = (bf16[1,1,4,192,2048]{4,3,2,1,0:T(8,128)(2,1)}, bf16[1,1,4,192,2048]{4,3,2,1,0:T(8,128)(2,1)}, u32[]{:S(2)}, u32[]{:S(2)}) collective-permute-start(bf16[1,1,4,192,2048]{4,3,2,1,0:T(8,128)(2,1)} %param.12), channel_id=1, source_target_pairs={{0,224},{32,0},{64,32},{96,64},{128,96},{160,128},{192,160},{224,1... | collective-permute-start | bytes 9437192 | tf_op jit(solution)/shard_map/ppermute | solution.py:20
  175.4 1.6 copy-start.7
  186.0 21.2 %copy-start.5 = (bf16[2,192,2048]{2,1,0:T(8,128)(2,1)S(1)}, bf16[2,192,2048]{2,1,0:T(8,128)(2,1)}, u32[]{:S(2)}) copy-start(bf16[2,192,2048]{2,1,0:T(8,128)(2,1)} %multiply_convert_fusion) | copy-start | bytes 4718596
  224.9 4.5 copy-start
  236.4 5.9 %copy-start.2 = (f32[2,192,4,4,32]{1,4,3,2,0:T(8,128)S(1)}, f32[2,192,4,4,32]{1,4,3,2,0:T(8,128)}, u32[]{:S(2)}) copy-start(f32[2,192,4,4,32]{1,4,3,2,0:T(8,128)} %copy.54) | copy-start | bytes 2359300
  236.4 5.9 %copy-start.3 = (f32[2,192,4,4,32]{1,4,3,2,0:T(8,128)S(1)}, f32[2,192,4,4,32]{1,4,3,2,0:T(8,128)}, u32[]{:S(2)}) copy-start(f32[2,192,4,4,32]{1,4,3,2,0:T(8,128)} %copy.53) | copy-start | bytes 2359300
  249.9 2.4 copy-start.12
  269.0 1.3 copy-start.10
  270.4 1.2 copy-start.4
  271.8 4.5 copy-start.11
  276.3 5.7 %copy-start.1 = (bf16[1024,2048]{1,0:T(8,128)(2,1)S(1)}, bf16[1024,2048]{1,0:T(8,128)(2,1)}, u32[]{:S(2)}) copy-start(bf16[1024,2048]{1,0:T(8,128)(2,1)} %convolution_convert_fusion.1) | copy-start | bytes 12582916
  294.4 160.1 %copy-start.6 = (bf16[1,80,2048]{2,1,0:T(8,128)(2,1)S(1)}, bf16[1,80,2048]{2,1,0:T(8,128)(2,1)}, u32[]{:S(2)}) copy-start(bf16[1,80,2048]{2,1,0:T(8,128)(2,1)} %param.8) | copy-start | bytes 983044
  294.4 160.1 %copy-start.8 = (f32[1,80,2048]{2,1,0:T(8,128)S(1)}, f32[1,80,2048]{2,1,0:T(8,128)}, u32[]{:S(2)}) copy-start(f32[1,80,2048]{2,1,0:T(8,128)} %param.10) | copy-start | bytes 1966084
  294.4 160.1 %copy-start.9 = (f32[1,80,2048]{2,1,0:T(8,128)S(1)}, f32[1,80,2048]{2,1,0:T(8,128)}, u32[]{:S(2)}) copy-start(f32[1,80,2048]{2,1,0:T(8,128)} %param.9) | copy-start | bytes 1966084
Sparse Core Ops, SparseCore 0:
  10.8 196.3 all-gather.1
  294.5 159.9 reduce-scatter.1
where the time goes:
time: 468 us; the launch traced here: 464 us
  waiting for transfers between devices  343 us (73%)
  local copies, waits for them, and re-layouts  42.2 us (9%)
  matrix products  31.9 us (7%)
  other arithmetic  29.7 us (6%)
  between operations  14.6 us (3%)
    ppermute x2, waiting for transfers between devices, shifted(): return lax.ppermute(value, axis, pairs)  162 us
    reduce_scatter x1, waiting for transfers between devices, shards(): lax.psum_scatter(local_grad, 'dp', scatter_dimension=0, tiled=True)  160 us
    all_gather x1, waiting for transfers between devices, shards(): gathered = lax.all_gather(params, 'dp', axis=1, tiled=True)  19.8 us
    add_any x1, other arithmetic, attention_branch(): weights[:query_total_width + 2 * key_value_width]  12.3 us
    unnamed x30, local copies, waits for them, and re-layouts  11 us
    dot_general x2, matrix products, attention_branch(): lax.dot_general(normed, weights[:query_total_width + 2 * key_value_width]...  10.7 us
    dot_general x2, matrix products, attention_branch(): jnp.dot(context, weights[query_total_width + 2 * key_value_width:], prefe...  10.4 us
  transfers between devices with their start and end apart: 4, of which 3 were waited for; matrix products, arithmetic and copies ran while one was open for 3% of the time, Pallas kernels for 0%

commit v1 on v0

v1 whole, which is shorter than its diff:
```python
import functools

import jax
import jax.numpy as jnp
import numpy as np
from jax import lax
from jax.experimental import pallas as pl
from jax.experimental.pallas import tpu as pltpu
from jax.sharding import PartitionSpec as P

HEAD_SIZE = 64
QUERY_HEADS = 16
KEY_VALUE_HEADS = 4
STEP = 100
SEQ = 192
LOG = 4
MB = 2
PROWS = 2560

N_SECTION = 8
N_DP = 32
N_Z = 8
CHUNK = 64
PER_Z = 5
LOCAL = 20
SHARD = 80
PIECE = 16
PIECES = SHARD // PIECE
Q_ROWS = 512
K_AT = 512
V_AT = 640
O_AT = 768
QKV_BLOCKS = 12

rope_base = 500000.0
learn_rate = 0.0003
decay_rate = 0.1

MESH = pl.DeviceIdType.MESH
BF16 = jnp.bfloat16
F32 = jnp.float32


def nn(a, b):
    return lax.dot_general(a, b, (((1,), (0,)), ((), ())), preferred_element_type=F32)


def nt(a, b):
    return lax.dot_general(a, b, (((1,), (1,)), ((), ())), preferred_element_type=F32)


def core_of(block):
    return jnp.where(
        block < 16,
        lax.div(block, 8),
        jnp.where(block < 24, lax.rem(lax.div(block - 16, 2), 2), lax.div(block - 24, 8)),
    )


def place_of(block):
    return jnp.where(
        block < 16,
        lax.rem(block, 8),
        jnp.where(
            block < 24,
            8 + 2 * lax.div(block - 16, 4) + lax.rem(block - 16, 2),
            12 + lax.rem(block - 24, 8),
        ),
    )


def kernel(
    params_hbm,
    sent_hbm,
    back_hbm,
    ids_ref,
    cos_ref,
    sin_ref,
    grad_ref,
    shard,
    sent,
    back,
    ids_next,
    ids_prev,
    ids_one,
    ids_two,
    weights,
    acts,
    picked,
    proj,
    dctx,
    lhs,
    total,
    stage,
    from_low,
    from_high,
    final,
    sem_local,
    sem_ids,
    sem_ids_send,
    sem_ids_recv,
    first_send,
    gather_up,
    gather_down,
    gather_recv,
    norm_send,
    norm_recv,
    pick_send,
    pick_recv,
    pass_send,
    pass_recv,
    sum_send,
    low_recv,
    high_recv,
    final_send,
    final_recv,
):
    section = lax.axis_index("section")
    dp = lax.axis_index("dp")
    z = lax.div(dp, 4)
    core = lax.rem(dp, 2)
    other = 1 - core
    owner_y = lax.rem(lax.div(dp, 2), 2)
    sibling = dp + 1 - 2 * core
    up = lax.rem(dp + 4, N_DP)
    down = lax.rem(dp + N_DP - 4, N_DP)
    before = lax.rem(section + N_SECTION - 1, N_SECTION)
    after = lax.rem(section + 1, N_SECTION)
    before_two = lax.rem(section + N_SECTION - 2, N_SECTION)
    after_two = lax.rem(section + 2, N_SECTION)
    width = weights.shape[2]

    loads = [
        pltpu.make_async_copy(params_hbm, shard, sem_local.at[0]),
        pltpu.make_async_copy(sent_hbm, sent, sem_local.at[1]),
        pltpu.make_async_copy(back_hbm, back, sem_local.at[2]),
    ]
    for load in loads:
        load.start()

    barrier = pltpu.get_barrier_semaphore()
    peers = [(section, sibling), (section, up), (section, down), (before_two, dp), (after_two, dp)]
    for quarter in range(4):
        peers.append((before, 4 * z + quarter))
        peers.append((after, 4 * z + quarter))
    for peer in peers:
        pl.semaphore_signal(barrier, inc=1, device_id=peer, device_id_type=MESH)
    pl.semaphore_wait(barrier, len(peers))

    id_copies = [
        pltpu.make_async_remote_copy(
            src_ref=ids_ref,
            dst_ref=ids_next,
            send_sem=sem_ids_send.at[0],
            recv_sem=sem_ids_recv.at[0],
            device_id=(before, dp),
            device_id_type=MESH,
        ),
        pltpu.make_async_remote_copy(
            src_ref=ids_ref,
            dst_ref=ids_prev,
            send_sem=sem_ids_send.at[1],
            recv_sem=sem_ids_recv.at[1],
            device_id=(after, dp),
            device_id_type=MESH,
        ),
    ]
    for copy in id_copies:
        copy.start()

    loads[0].wait()

    def first_copy(piece, half):
        row = SHARD * dp + PIECE * piece
        block = lax.div(row, CHUNK)
        return pltpu.make_async_remote_copy(
            src_ref=shard.at[pl.ds(PIECE * piece, PIECE)],
            dst_ref=weights.at[place_of(block), pl.ds(pl.multiple_of(lax.rem(row, CHUNK), PIECE), PIECE)],
            send_sem=first_send.at[2 * piece + half],
            recv_sem=gather_recv.at[place_of(block)],
            device_id=(before, 4 * z + 2 * half + core_of(block)),
            device_id_type=MESH,
        )

    for piece in range(PIECES):
        for half in range(2):
            first_copy(piece, half).start()

    pick_copies = []
    norm_copies = []
    id_copies[0].wait_recv()
    to_one = pltpu.make_async_copy(ids_next, ids_one, sem_ids.at[0])
    to_one.start()
    to_one.wait()
    id_copies[1].wait_recv()
    to_two = pltpu.make_async_copy(ids_prev, ids_two, sem_ids.at[1])
    to_two.start()
    to_two.wait()

    loads[2].wait()
    for m in range(MB):
        wanted = ids_two[m, 0]

        def pick_rows(n, carry, m=m, wanted=wanted):
            rows = pl.ds(pl.multiple_of(n * 16, 16), 16)
            picked[m, rows, :] = back[wanted, rows, :]
            return carry

        lax.fori_loop(0, SEQ // 16, pick_rows, 0)
        pick_copies.append(
            pltpu.make_async_remote_copy(
                src_ref=picked.at[m],
                dst_ref=acts.at[1, 2 * core + m],
                send_sem=pick_send.at[m],
                recv_sem=pick_recv.at[m],
                device_id=(before_two, dp),
                device_id_type=MESH,
            )
        )
        pick_copies[m].start()

    loads[1].wait()
    for m in range(MB):
        wanted = ids_one[m, 0]

        def norm_rows(n, carry, m=m, wanted=wanted):
            rows = pl.ds(pl.multiple_of(n * 16, 16), 16)
            value = sent[wanted, rows, :].astype(F32)
            scaling = lax.rsqrt(jnp.mean(value * value, axis=-1, keepdims=True) + 1e-05)
            acts[0, 2 * core + m, rows, :] = (value * scaling).astype(BF16)
            return carry

        lax.fori_loop(0, SEQ // 16, norm_rows, 0)
        norm_copies.append(
            pltpu.make_async_remote_copy(
                src_ref=acts.at[0, 2 * core + m],
                dst_ref=acts.at[0, 2 * core + m],
                send_sem=norm_send.at[m],
                recv_sem=norm_recv.at[m],
                device_id=(section, sibling),
                device_id_type=MESH,
            )
        )
        norm_copies[m].start()

    def gather_copy(place, going_up):
        return pltpu.make_async_remote_copy(
            src_ref=weights.at[place],
            dst_ref=weights.at[place],
            send_sem=(gather_up if going_up else gather_down).at[place],
            recv_sem=gather_recv.at[place],
            device_id=(section, up if going_up else down),
            device_id_type=MESH,
        )

    def gather_step(n):
        m = n - PER_Z
        middle = jnp.logical_and(n >= PER_Z, n < 35)
        away = jnp.where(n < PER_Z, 0, jnp.where(middle, 1 + lax.div(m, 10), 4))
        which = jnp.where(n < PER_Z, n, jnp.where(middle, lax.div(lax.rem(m, 10), 2), n - 35))
        rising = jnp.logical_and(middle, lax.rem(m, 2) == 0)
        home = lax.rem(jnp.where(rising, z - away, z + away) + N_Z, N_Z)
        block = PER_Z * home + which
        odd = lax.rem(block, 2)
        mine = core_of(block) == core
        start = n < PER_Z
        falling = jnp.logical_and(middle, jnp.logical_not(rising))
        send_up = jnp.logical_or(start, jnp.logical_and(rising, away < 4 - odd))
        send_down = jnp.logical_or(start, jnp.logical_and(falling, away < 3 + odd))
        return place_of(block), mine, jnp.logical_and(mine, send_up), jnp.logical_and(mine, send_down)

    def gather(n, carry):
        place, mine, send_up, send_down = gather_step(n)

        @pl.when(mine)
        def _():
            gather_copy(place, True).wait_recv()

        @pl.when(send_up)
        def _():
            gather_copy(place, True).start()

        @pl.when(send_down)
        def _():
            gather_copy(place, False).start()

        return carry

    lax.fori_loop(0, 40, gather, 0)

    pass_copies = []
    for m in range(MB):
        pick_copies[m].wait_recv()
        pass_copies.append(
            pltpu.make_async_remote_copy(
                src_ref=acts.at[1, 2 * core + m],
                dst_ref=acts.at[1, 2 * core + m],
                send_sem=pass_send.at[m],
                recv_sem=pass_recv.at[m],
                device_id=(section, sibling),
                device_id_type=MESH,
            )
        )
        pass_copies[m].start()
    for m in range(MB):
        norm_copies[m].wait_recv()

    def project(n, carry):
        batch, part = lax.div(n, 3), lax.rem(n, 3)
        rows = weights[pl.ds(4 * part, 4)].reshape(4 * CHUNK, width)
        proj[batch, pl.ds(pl.multiple_of(part * 256, 256), 256), :] = nt(rows, acts[0, batch])
        return carry

    lax.fori_loop(0, 12, project, 0)

    for m in range(MB):
        pass_copies[m].wait_recv()

    def cotangent(n, carry):
        batch, part = lax.div(n, 2), lax.rem(n, 2)
        rows = weights[pl.ds(QKV_BLOCKS + 4 * part, 4)].reshape(4 * CHUNK, width)
        dctx[batch, pl.ds(pl.multiple_of(part * 256, 256), 256), :] = nt(rows, acts[1, batch]).astype(BF16)
        return carry

    lax.fori_loop(0, 8, cotangent, 0)

    cosine, sine = cos_ref[...], sin_ref[...]
    half = HEAD_SIZE // 2

    def rotate(value):
        a, b = value[:half], value[half:]
        return jnp.concatenate([a * cosine - b * sine, b * cosine + a * sine], axis=0)

    def rotate_back(value):
        a, b = value[:half], value[half:]
        return jnp.concatenate([a * cosine + b * sine, b * cosine - a * sine], axis=0)

    def attention(n, carry):
        batch, group = lax.div(n, 2), lax.rem(n, 2)
        key_rows = pl.ds(pl.multiple_of(K_AT + HEAD_SIZE * group, HEAD_SIZE), HEAD_SIZE)
        value_rows = pl.ds(pl.multiple_of(V_AT + HEAD_SIZE * group, HEAD_SIZE), HEAD_SIZE)
        key_t = rotate(proj[batch, key_rows, :])
        value_t = proj[batch, value_rows, :]
        key = key_t.T.astype(BF16)
        value = value_t.T.astype(BF16)
        key_t = key_t.astype(BF16)
        value_t = value_t.astype(BF16)
        kept = lax.broadcasted_iota(jnp.int32, (SEQ, SEQ), 0) <= lax.broadcasted_iota(jnp.int32, (SEQ, SEQ), 1)
        dkey = jnp.zeros((HEAD_SIZE, SEQ), F32)
        dvalue = jnp.zeros((HEAD_SIZE, SEQ), F32)
        for head in range(4):
            first = 256 * group + HEAD_SIZE * head
            rows = pl.ds(pl.multiple_of(first, HEAD_SIZE), HEAD_SIZE)
            query_t = (rotate(proj[batch, rows, :]) * HEAD_SIZE**-0.5).astype(BF16)
            scores = jnp.where(kept, nn(key, query_t), -1e30)
            raised = jnp.exp(scores - jnp.max(scores, axis=0, keepdims=True))
            probs = raised * (1.0 / jnp.sum(raised, axis=0, keepdims=True))
            probs_b = probs.astype(BF16)
            context_rows = pl.ds(pl.multiple_of(O_AT + first, HEAD_SIZE), HEAD_SIZE)
            lhs[batch, context_rows, :] = nn(value_t, probs_b).astype(BF16)
            cot = dctx[batch, rows, :]
            dprobs = nn(value, cot)
            dvalue = dvalue + nt(cot, probs_b)
            delta = jnp.sum(dprobs * probs, axis=0, keepdims=True)
            dscores = (probs * (dprobs - delta)).astype(BF16)
            dquery = nn(key_t, dscores) * HEAD_SIZE**-0.5
            lhs[batch, rows, :] = rotate_back(dquery).astype(BF16)
            dkey = dkey + nt(query_t, dscores)
        lhs[batch, key_rows, :] = rotate_back(dkey).astype(BF16)
        lhs[batch, value_rows, :] = dvalue.astype(BF16)
        return carry

    lax.fori_loop(0, 8, attention, 0)

    def sum_copy(place, going_up):
        landing, arrived = (from_low, low_recv) if going_up else (from_high, high_recv)
        return pltpu.make_async_remote_copy(
            src_ref=stage.at[place],
            dst_ref=landing.at[place],
            send_sem=sum_send.at[place],
            recv_sem=arrived.at[place],
            device_id=(section, up if going_up else down),
            device_id_type=MESH,
        )

    def final_copy(which, quarter):
        row = CHUNK * (PER_Z * z + which) + PIECE * quarter
        inside = row - PER_Z * CHUNK * z
        keeper = lax.div(inside, SHARD)
        offset = pl.multiple_of(inside - SHARD * keeper, PIECE)
        return pltpu.make_async_remote_copy(
            src_ref=stage.at[place_of(PER_Z * z + which), pl.ds(PIECE * quarter, PIECE)],
            dst_ref=final.at[owner_y, pl.ds(offset, PIECE)],
            send_sem=final_send.at[4 * which + quarter],
            recv_sem=final_recv.at[owner_y],
            device_id=(after, 4 * z + keeper),
            device_id_type=MESH,
        )

    def sum_step(n):
        m = n - PER_Z
        middle = jnp.logical_and(n >= PER_Z, n < 35)
        last = n >= 35
        away = jnp.where(n < PER_Z, 4, jnp.where(middle, 3 - lax.div(m, 10), 0))
        which = jnp.where(n < PER_Z, n, jnp.where(middle, lax.div(lax.rem(m, 10), 2), n - 35))
        falling = jnp.logical_and(middle, lax.rem(m, 2) == 1)
        home = lax.rem(jnp.where(falling, z - away, z + away) + N_Z, N_Z)
        block = PER_Z * home + which
        odd = lax.rem(block, 2)
        mine = core_of(block) == core
        rises = jnp.where(middle, jnp.logical_not(falling), odd == 0)
        has_low = jnp.logical_or(last, jnp.logical_and(rises, away < 4 - odd))
        has_high = jnp.logical_or(last, jnp.logical_and(jnp.logical_not(rises), away < 3 + odd))
        go_up = jnp.logical_and(mine, jnp.logical_and(rises, jnp.logical_not(last)))
        go_down = jnp.logical_and(mine, jnp.logical_and(jnp.logical_not(rises), jnp.logical_not(last)))
        return place_of(block), which, mine, has_low, has_high, go_up, go_down, jnp.logical_and(mine, last)

    def reduce(n, carry):
        place, which, mine, has_low, has_high, go_up, go_down, last = sum_step(n)

        @pl.when(mine)
        def _():
            rows = pl.ds(pl.multiple_of(place * CHUNK, CHUNK), CHUNK)
            side = jnp.where(place >= QKV_BLOCKS, 1, 0)
            for tile in range(4):
                columns = slice(tile * width // 4, (tile + 1) * width // 4)
                value = nn(lhs[0, rows, :], acts[side, 0, :, columns])
                for batch in range(1, 2 * MB):
                    value = value + nn(lhs[batch, rows, :], acts[side, batch, :, columns])
                total[:, columns] = value

        @pl.when(jnp.logical_and(mine, has_low))
        def _():
            sum_copy(place, True).wait_recv()
            total[...] += from_low[place].astype(F32)

        @pl.when(jnp.logical_and(mine, has_high))
        def _():
            sum_copy(place, False).wait_recv()
            total[...] += from_high[place].astype(F32)

        @pl.when(mine)
        def _():
            stage[place] = total[...].astype(BF16)

        @pl.when(go_up)
        def _():
            sum_copy(place, True).start()

        @pl.when(go_down)
        def _():
            sum_copy(place, False).start()

        @pl.when(last)
        def _():
            for quarter in range(CHUNK // PIECE):
                final_copy(which, quarter).start()

        return carry

    lax.fori_loop(0, 40, reduce, 0)

    for copy in id_copies + pick_copies + norm_copies + pass_copies:
        copy.wait_send()
    for piece in range(PIECES):
        for half_y in range(2):
            first_copy(piece, half_y).wait_send()

    def drain(n, carry):
        place, _, send_up, send_down = gather_step(n)

        @pl.when(send_up)
        def _():
            gather_copy(place, True).wait_send()

        @pl.when(send_down)
        def _():
            gather_copy(place, False).wait_send()

        place, which, _, _, _, go_up, go_down, last = sum_step(n)

        @pl.when(jnp.logical_or(go_up, go_down))
        def _():
            sum_copy(place, True).wait_send()

        @pl.when(last)
        def _():
            for quarter in range(CHUNK // PIECE):
                final_copy(which, quarter).wait_send()

        return carry

    lax.fori_loop(0, 40, drain, 0)

    for source in range(2):
        pltpu.make_async_remote_copy(
            src_ref=final.at[source],
            dst_ref=final.at[source],
            send_sem=final_send.at[0],
            recv_sem=final_recv.at[source],
            device_id=(after, dp),
            device_id_type=MESH,
        ).wait_recv()
    grad_ref[...] = final[0].astype(F32) + final[1].astype(F32)


def summed_gradient(params, sent, back, ids):
    width = params.shape[-1]
    frequency = rope_base ** (-np.arange(HEAD_SIZE // 2, dtype=np.float64) * 2.0 / HEAD_SIZE)
    angles = frequency[:, None] * np.arange(SEQ, dtype=np.float64)[None, :]
    cosine = jnp.asarray(np.cos(angles), F32)
    sine = jnp.asarray(np.sin(angles), F32)
    wide_ids = jnp.broadcast_to(ids.reshape(MB, 1), (MB, 128))
    wide_ids = jnp.concatenate([wide_ids, jnp.zeros((8 - MB, 128), jnp.int32)], axis=0)
    dma = pltpu.SemaphoreType.DMA
    in_vmem = pl.BlockSpec(memory_space=pltpu.VMEM)
    anywhere = pl.BlockSpec(memory_space=pl.ANY)
    return pl.pallas_call(
        kernel,
        out_shape=jax.ShapeDtypeStruct((SHARD, width), F32),
        in_specs=[anywhere, anywhere, anywhere, in_vmem, in_vmem, in_vmem],
        out_specs=in_vmem,
        scratch_shapes=[
            pltpu.VMEM((SHARD, width), BF16),
            pltpu.VMEM((LOG, SEQ, width), BF16),
            pltpu.VMEM((LOG, SEQ, width), BF16),
            pltpu.VMEM((8, 128), jnp.int32),
            pltpu.VMEM((8, 128), jnp.int32),
            pltpu.SMEM((8, 128), jnp.int32),
            pltpu.SMEM((8, 128), jnp.int32),
            pltpu.VMEM((LOCAL, CHUNK, width), BF16),
            pltpu.VMEM((2, 2 * MB, SEQ, width), BF16),
            pltpu.VMEM((MB, SEQ, width), BF16),
            pltpu.VMEM((2 * MB, O_AT, SEQ), F32),
            pltpu.VMEM((2 * MB, Q_ROWS, SEQ), BF16),
            pltpu.VMEM((2 * MB, LOCAL * CHUNK, SEQ), BF16),
            pltpu.VMEM((CHUNK, width), F32),
            pltpu.VMEM((LOCAL, CHUNK, width), BF16),
            pltpu.VMEM((LOCAL, CHUNK, width), BF16),
            pltpu.VMEM((LOCAL, CHUNK, width), BF16),
            pltpu.VMEM((2, SHARD, width), BF16),
            dma((3,)),
            dma((2,)),
            dma((2,)),
            dma((2,)),
            dma((2 * PIECES,)),
            dma((LOCAL,)),
            dma((LOCAL,)),
            dma((LOCAL,)),
            dma((MB,)),
            dma((MB,)),
            dma((MB,)),
            dma((MB,)),
            dma((MB,)),
            dma((MB,)),
            dma((LOCAL,)),
            dma((LOCAL,)),
            dma((LOCAL,)),
            dma((4 * PER_Z,)),
            dma((2,)),
        ],
        compiler_params=pltpu.CompilerParams(
            collective_id=0, has_side_effects=True, vmem_limit_bytes=60 * 1024 * 1024
        ),
    )(params, sent, back, wide_ids, cosine, sine)


def apply_adam(weights, first_moment, second_moment, gradient):
    first_new = 0.9 * first_moment + 0.1 * gradient
    second_new = 0.999 * second_moment + 0.001 * gradient * gradient
    fix_first = 1.0 - 0.9**STEP
    fix_second = 1.0 - 0.999**STEP
    update = first_new / fix_first / (jnp.sqrt(second_new / fix_second) + 1e-08)
    current = weights.astype(F32)
    renewed = (current - learn_rate * (update + decay_rate * current)).astype(BF16)
    return (renewed, first_new, second_new)


def shards(params, moment_one, moment_two, sent_rows, back_rows, slot_ids):
    summed = summed_gradient(params[0], sent_rows[0, 0], back_rows[0, 0], slot_ids[0, 0])
    renewed, first_new, second_new = apply_adam(params[0], moment_one[0], moment_two[0], summed / N_DP)
    return (renewed[None], first_new[None], second_new[None])


def solution(mesh):
    in_specs = (
        P("section", "dp", None),
        P("section", "dp", None),
        P("section", "dp", None),
        P("section", "dp", None, None, None),
        P("section", "dp", None, None, None),
        P("section", "dp", None),
    )
    out_specs = (P("section", "dp", None), P("section", "dp", None), P("section", "dp", None))
    return jax.shard_map(shards, mesh=mesh, in_specs=in_specs, out_specs=out_specs, check_vma=False)
```

time: 468 us -> 172 us (0.37)
  the two profiles are of different devices: /device:TPU:6 before, /device:TPU:48 now
where the time goes in v1:
time: 172 us
  Pallas kernels  167 us (97%)
  other arithmetic  2.78 us (2%)
    pallas_call x1, Pallas kernels, summed_gradient(): pl.pallas_call(kernel, out_shape=jax.ShapeDtypeStruct((SHARD, width), F32...  167 us

profile of v1, /device:TPU:48, one launch (start us, length us, event | category | flops | bytes accessed | tf_op | source)
XLA Modules:
  0.0 171.5 jit_solution(3036654258497730181)
XLA Ops:
  0.6 0.7 concatenate.5
  1.3 0.7 concatenate.6.ids_ref
  2.0 0.0 copy-start
  2.0 0.0 copy-start.1
  2.0 0.0 copy-start.2
  2.0 166.7 %shard_map.103 = f32[80,2048]{1,0:T(8,128)} custom-call(bf16[80,2048]{1,0:T(8,128)(2,1)} %bitcast.25, bf16[4,192,2048]{2,1,0:T(8,128)(2,1)} %bitcast.23, bf16[4,192,2048]{2,1,0:T(8,128)(2,1)} %bitcast.24, s32[8,128]{1,0:T(8,128)} %concatenate.6.ids_ref, f32[32,192]{1,0:T(8,128)} %constant.30.clone.cos_ref, f32[32,192]{1,0:T(8,128)} %constant.31.clone.sin_ref), custom_call_target="tpu_custom_call" | custom-call | tf_op jit(solution)/shard_map/pallas_call | solution.py:518
  168.7 0.0 copy-done
  168.7 0.0 copy-done.1
  168.7 0.0 copy-done.2
  168.7 2.8 %fusion.5 = (f32[1,80,2048]{2,1,0:T(8,128)}, bf16[1,80,2048]{2,1,0:T(8,128)(2,1)}, f32[1,80,2048]{2,1,0:T(8,128)}) fusion(f32[80,2048]{1,0:T(8,128)} %shard_map.103, f32[1,80,2048]{2,1,0:T(8,128)S(1)} %copy-done.1, f32[1,80,2048]{2,1,0:T(8,128)S(1)} %copy-done.2, bf16[1,80,2048]{2,1,0:T(8,128)(2,1)S(1)} %copy-done), kind=kLoop, calls=%fused_computation.9 | loop fusion | flops 2949120 | bytes 3932160 | tf_op jit(solution)/shard_map/broadcast_in_dim | solution.py:582
Async XLA Ops:
  2.0 166.7 %copy-start = (bf16[1,80,2048]{2,1,0:T(8,128)(2,1)S(1)}, bf16[1,80,2048]{2,1,0:T(8,128)(2,1)}, u32[]{:S(2)}) copy-start(bf16[1,80,2048]{2,1,0:T(8,128)(2,1)} %param.8) | copy-start | bytes 983044
  2.0 166.8 %copy-start.1 = (f32[1,80,2048]{2,1,0:T(8,128)S(1)}, f32[1,80,2048]{2,1,0:T(8,128)}, u32[]{:S(2)}) copy-start(f32[1,80,2048]{2,1,0:T(8,128)} %param.10) | copy-start | bytes 1966084
  2.0 166.8 %copy-start.2 = (f32[1,80,2048]{2,1,0:T(8,128)S(1)}, f32[1,80,2048]{2,1,0:T(8,128)}, u32[]{:S(2)}) copy-start(f32[1,80,2048]{2,1,0:T(8,128)} %param.9) | copy-start | bytes 1966084

commit v2 on v1

--- a/solution.py
+++ b/solution.py
@@ -1,5 +1,3 @@
-import functools
-
 import jax
 import jax.numpy as jnp
 import numpy as np
@@ -24,6 +22,7 @@
 PER_Z = 5
 LOCAL = 20
 SHARD = 80
+LEAD = 8
 PIECE = 16
 PIECES = SHARD // PIECE
 Q_ROWS = 512
@@ -67,6 +66,19 @@
             12 + lax.rem(block - 24, 8),
         ),
     )
+
+
+def by_y(home, which):
+    even = lax.rem(home, 2) == 0
+    stays = jnp.logical_or(which == 2, which == jnp.where(even, 0, 4))
+    return jnp.logical_not(stays)
+
+
+def more_down(home, which):
+    even = lax.rem(home, 2) == 0
+    lone = which == jnp.where(even, 1, 3)
+    second = jnp.logical_or(which == 4, which == jnp.where(even, 2, 1))
+    return jnp.where(lone, lax.rem(lax.div(home, 2), 2), jnp.where(second, 1, 0))
 
 
 def kernel(
@@ -85,6 +97,7 @@
     ids_one,
     ids_two,
     weights,
+    relay,
     acts,
     picked,
     proj,
@@ -92,6 +105,7 @@
     lhs,
     total,
     stage,
+    given,
     from_low,
     from_high,
     final,
@@ -103,8 +117,13 @@
     gather_up,
     gather_down,
     gather_recv,
-    norm_send,
-    norm_recv,
+    relay_up,
+    relay_down,
+    relay_out,
+    relay_recv,
+    own_local,
+    own_send,
+    own_recv,
     pick_send,
     pick_recv,
     pass_send,
@@ -112,6 +131,8 @@
     sum_send,
     low_recv,
     high_recv,
+    give_send,
+    give_recv,
     final_send,
     final_recv,
 ):
@@ -119,8 +140,9 @@
     dp = lax.axis_index("dp")
     z = lax.div(dp, 4)
     core = lax.rem(dp, 2)
-    other = 1 - core
-    owner_y = lax.rem(lax.div(dp, 2), 2)
+    my_y = lax.rem(lax.div(dp, 2), 2)
+    odd_section = lax.rem(section, 2)
+    partner = section + 1 - 2 * odd_section
     sibling = dp + 1 - 2 * core
     up = lax.rem(dp + 4, N_DP)
     down = lax.rem(dp + N_DP - 4, N_DP)
@@ -139,10 +161,10 @@
         load.start()
 
     barrier = pltpu.get_barrier_semaphore()
-    peers = [(section, sibling), (section, up), (section, down), (before_two, dp), (after_two, dp)]
+    beyond = jnp.where(odd_section == 0, before, after)
+    peers = [(section, sibling), (section, up), (section, down), (before_two, dp), (after_two, dp), (beyond, dp)]
     for quarter in range(4):
-        peers.append((before, 4 * z + quarter))
-        peers.append((after, 4 * z + quarter))
+        peers.append((partner, 4 * z + quarter))
     for peer in peers:
         pl.semaphore_signal(barrier, inc=1, device_id=peer, device_id_type=MESH)
     pl.semaphore_wait(barrier, len(peers))
@@ -178,16 +200,51 @@
             dst_ref=weights.at[place_of(block), pl.ds(pl.multiple_of(lax.rem(row, CHUNK), PIECE), PIECE)],
             send_sem=first_send.at[2 * piece + half],
             recv_sem=gather_recv.at[place_of(block)],
-            device_id=(before, 4 * z + 2 * half + core_of(block)),
-            device_id_type=MESH,
-        )
+            device_id=(partner, 4 * z + 2 * half + core_of(block)),
+            device_id_type=MESH,
+        )
+
+    def relay_piece(piece, local):
+        row = SHARD * dp + PIECE * piece
+        block = lax.div(row, CHUNK)
+        source = shard.at[pl.ds(PIECE * piece, PIECE)]
+        target = relay.at[place_of(block), pl.ds(pl.multiple_of(lax.rem(row, CHUNK), PIECE), PIECE)]
+        arrived = relay_recv.at[place_of(block)]
+        if local:
+            return pltpu.make_async_copy(source, target, arrived)
+        return pltpu.make_async_remote_copy(
+            src_ref=source,
+            dst_ref=target,
+            send_sem=first_send.at[2 * piece],
+            recv_sem=arrived,
+            device_id=(section, sibling),
+            device_id_type=MESH,
+        )
+
+    def piece_way(piece):
+        block = lax.div(SHARD * dp + PIECE * piece, CHUNK)
+        across = by_y(z, block - PER_Z * z)
+        here = core_of(block) == core
+        return across, jnp.logical_and(across, here), jnp.logical_and(across, jnp.logical_not(here))
 
     for piece in range(PIECES):
-        for half in range(2):
-            first_copy(piece, half).start()
-
-    pick_copies = []
-    norm_copies = []
+        across, here, there = piece_way(piece)
+
+        @pl.when(jnp.logical_not(across))
+        def _(piece=piece):
+            for half in range(2):
+                first_copy(piece, half).start()
+
+        @pl.when(here)
+        def _(piece=piece):
+            relay_piece(piece, True).start()
+
+        @pl.when(there)
+        def _(piece=piece):
+            relay_piece(piece, False).start()
+
+    stays, leaves = odd_section, 1 - odd_section
+    target_section = jnp.where(odd_section == 0, before_two, after_two)
     id_copies[0].wait_recv()
     to_one = pltpu.make_async_copy(ids_next, ids_one, sem_ids.at[0])
     to_one.start()
@@ -196,52 +253,49 @@
     to_two = pltpu.make_async_copy(ids_prev, ids_two, sem_ids.at[1])
     to_two.start()
     to_two.wait()
-
+    loads[1].wait()
     loads[2].wait()
+    own_copies = []
+    own_locals = []
+    pick_copies = []
     for m in range(MB):
-        wanted = ids_two[m, 0]
-
-        def pick_rows(n, carry, m=m, wanted=wanted):
+        wanted_one, wanted_two = ids_one[m, 0], ids_two[m, 0]
+
+        def pick_rows(n, carry, m=m, wanted_one=wanted_one, wanted_two=wanted_two):
             rows = pl.ds(pl.multiple_of(n * 16, 16), 16)
-            picked[m, rows, :] = back[wanted, rows, :]
+            value = sent[wanted_one, rows, :].astype(F32)
+            scaling = lax.rsqrt(jnp.mean(value * value, axis=-1, keepdims=True) + 1e-05)
+            picked[0, m, rows, :] = (value * scaling).astype(BF16)
+            picked[1, m, rows, :] = back[wanted_two, rows, :]
             return carry
 
         lax.fori_loop(0, SEQ // 16, pick_rows, 0)
         pick_copies.append(
             pltpu.make_async_remote_copy(
-                src_ref=picked.at[m],
-                dst_ref=acts.at[1, 2 * core + m],
+                src_ref=picked.at[leaves, m],
+                dst_ref=acts.at[leaves, 2 * core + m],
                 send_sem=pick_send.at[m],
                 recv_sem=pick_recv.at[m],
-                device_id=(before_two, dp),
+                device_id=(target_section, dp),
                 device_id_type=MESH,
             )
         )
-        pick_copies[m].start()
-
-    loads[1].wait()
-    for m in range(MB):
-        wanted = ids_one[m, 0]
-
-        def norm_rows(n, carry, m=m, wanted=wanted):
-            rows = pl.ds(pl.multiple_of(n * 16, 16), 16)
-            value = sent[wanted, rows, :].astype(F32)
-            scaling = lax.rsqrt(jnp.mean(value * value, axis=-1, keepdims=True) + 1e-05)
-            acts[0, 2 * core + m, rows, :] = (value * scaling).astype(BF16)
-            return carry
-
-        lax.fori_loop(0, SEQ // 16, norm_rows, 0)
-        norm_copies.append(
+        own_copies.append(
             pltpu.make_async_remote_copy(
-                src_ref=acts.at[0, 2 * core + m],
-                dst_ref=acts.at[0, 2 * core + m],
-                send_sem=norm_send.at[m],
-                recv_sem=norm_recv.at[m],
+                src_ref=picked.at[stays, m],
+                dst_ref=acts.at[stays, 2 * core + m],
+                send_sem=own_send.at[m],
+                recv_sem=own_recv.at[m],
                 device_id=(section, sibling),
                 device_id_type=MESH,
             )
         )
-        norm_copies[m].start()
+        own_locals.append(
+            pltpu.make_async_copy(picked.at[stays, m], acts.at[stays, 2 * core + m], own_local.at[m])
+        )
+        pick_copies[m].start()
+        own_copies[m].start()
+        own_locals[m].start()
 
     def gather_copy(place, going_up):
         return pltpu.make_async_remote_copy(
@@ -250,6 +304,26 @@
             send_sem=(gather_up if going_up else gather_down).at[place],
             recv_sem=gather_recv.at[place],
             device_id=(section, up if going_up else down),
+            device_id_type=MESH,
+        )
+
+    def relay_copy(place, going_up):
+        return pltpu.make_async_remote_copy(
+            src_ref=relay.at[place],
+            dst_ref=relay.at[place],
+            send_sem=(relay_up if going_up else relay_down).at[place],
+            recv_sem=relay_recv.at[place],
+            device_id=(section, up if going_up else down),
+            device_id_type=MESH,
+        )
+
+    def relay_over(place, half):
+        return pltpu.make_async_remote_copy(
+            src_ref=relay.at[place],
+            dst_ref=weights.at[place],
+            send_sem=relay_out.at[LOCAL * half + place],
+            recv_sem=gather_recv.at[place],
+            device_id=(partner, 4 * z + 2 * half + core),
             device_id_type=MESH,
         )
 
@@ -261,28 +335,48 @@
         rising = jnp.logical_and(middle, lax.rem(m, 2) == 0)
         home = lax.rem(jnp.where(rising, z - away, z + away) + N_Z, N_Z)
         block = PER_Z * home + which
-        odd = lax.rem(block, 2)
+        odd = more_down(home, which)
         mine = core_of(block) == core
+        across = by_y(home, which)
+        mine_relay = jnp.logical_and(jnp.logical_and(mine, across), lax.div(which, 3) == my_y)
+        mine_ring = jnp.logical_and(mine, jnp.logical_not(across))
         start = n < PER_Z
         falling = jnp.logical_and(middle, jnp.logical_not(rising))
         send_up = jnp.logical_or(start, jnp.logical_and(rising, away < 4 - odd))
         send_down = jnp.logical_or(start, jnp.logical_and(falling, away < 3 + odd))
-        return place_of(block), mine, jnp.logical_and(mine, send_up), jnp.logical_and(mine, send_down)
+        return place_of(block), mine_ring, mine_relay, send_up, send_down
 
     def gather(n, carry):
-        place, mine, send_up, send_down = gather_step(n)
-
-        @pl.when(mine)
+        place, mine_ring, mine_relay, send_up, send_down = gather_step(n)
+
+        @pl.when(mine_ring)
         def _():
             gather_copy(place, True).wait_recv()
 
-        @pl.when(send_up)
+        @pl.when(jnp.logical_and(mine_ring, send_up))
         def _():
             gather_copy(place, True).start()
 
-        @pl.when(send_down)
+        @pl.when(jnp.logical_and(mine_ring, send_down))
         def _():
             gather_copy(place, False).start()
+
+        @pl.when(mine_relay)
+        def _():
+            relay_copy(place, True).wait_recv()
+
+        @pl.when(jnp.logical_and(mine_relay, send_up))
+        def _():
+            relay_copy(place, True).start()
+
+        @pl.when(jnp.logical_and(mine_relay, send_down))
+        def _():
+            relay_copy(place, False).start()
+
+        @pl.when(mine_relay)
+        def _():
+            for half_y in range(2):
+                relay_over(place, half_y).start()
 
         return carry
 
@@ -293,8 +387,8 @@
         pick_copies[m].wait_recv()
         pass_copies.append(
             pltpu.make_async_remote_copy(
-                src_ref=acts.at[1, 2 * core + m],
-                dst_ref=acts.at[1, 2 * core + m],
+                src_ref=acts.at[leaves, 2 * core + m],
+                dst_ref=acts.at[leaves, 2 * core + m],
                 send_sem=pass_send.at[m],
                 recv_sem=pass_recv.at[m],
                 device_id=(section, sibling),
@@ -302,8 +396,22 @@
             )
         )
         pass_copies[m].start()
+
+    def arrive(block, carry):
+        across = by_y(lax.div(block, PER_Z), lax.rem(block, PER_Z))
+
+        @pl.when(jnp.logical_and(across, core_of(block) == core))
+        def _():
+            gather_copy(place_of(block), True).wait_recv()
+
+        return carry
+
+    lax.fori_loop(0, 40, arrive, 0)
+
     for m in range(MB):
-        norm_copies[m].wait_recv()
+        own_locals[m].wait()
+        own_copies[m].wait_recv()
+        pass_copies[m].wait_recv()
 
     def project(n, carry):
         batch, part = lax.div(n, 3), lax.rem(n, 3)
@@ -312,9 +420,6 @@
         return carry
 
     lax.fori_loop(0, 12, project, 0)
-
-    for m in range(MB):
-        pass_copies[m].wait_recv()
 
     def cotangent(n, carry):
         batch, part = lax.div(n, 2), lax.rem(n, 2)
@@ -383,17 +488,55 @@
             device_id_type=MESH,
         )
 
+    def give_copy(place, which):
+        return pltpu.make_async_remote_copy(
+            src_ref=stage.at[place],
+            dst_ref=given.at[my_y, place],
+            send_sem=give_send.at[place],
+            recv_sem=give_recv.at[LOCAL * my_y + place],
+            device_id=(partner, 4 * z + 2 * lax.div(which, 3) + core),
+            device_id_type=MESH,
+        )
+
+    def keeper_of(which, quarter):
+        inside = CHUNK * which + PIECE * quarter
+        keeper = lax.div(inside, SHARD)
+        return keeper, lax.div(inside - SHARD * keeper, PIECE)
+
     def final_copy(which, quarter):
-        row = CHUNK * (PER_Z * z + which) + PIECE * quarter
-        inside = row - PER_Z * CHUNK * z
-        keeper = lax.div(inside, SHARD)
-        offset = pl.multiple_of(inside - SHARD * keeper, PIECE)
+        keeper, piece = keeper_of(which, quarter)
         return pltpu.make_async_remote_copy(
             src_ref=stage.at[place_of(PER_Z * z + which), pl.ds(PIECE * quarter, PIECE)],
-            dst_ref=final.at[owner_y, pl.ds(offset, PIECE)],
+            dst_ref=final.at[my_y, pl.ds(pl.multiple_of(PIECE * piece, PIECE), PIECE)],
             send_sem=final_send.at[4 * which + quarter],
-            recv_sem=final_recv.at[owner_y],
-            device_id=(after, 4 * z + keeper),
+            recv_sem=final_recv.at[PIECES * my_y + piece],
+            device_id=(partner, 4 * z + keeper),
+            device_id_type=MESH,
+        )
+
+    def relay_final(which, quarter, local):
+        _, piece = keeper_of(which, quarter)
+        source = given.at[0, place_of(PER_Z * z + which), pl.ds(PIECE * quarter, PIECE)]
+        target = final.at[0, pl.ds(pl.multiple_of(PIECE * piece, PIECE), PIECE)]
+        if local:
+            return pltpu.make_async_copy(source, target, final_recv.at[piece])
+        return pltpu.make_async_remote_copy(
+            src_ref=source,
+            dst_ref=target,
+            send_sem=final_send.at[4 * which + quarter],
+            recv_sem=final_recv.at[piece],
+            device_id=(section, sibling),
+            device_id_type=MESH,
+        )
+
+    def relay_sum_copy(place, going_up):
+        landing, arrived = (from_low, low_recv) if going_up else (from_high, high_recv)
+        return pltpu.make_async_remote_copy(
+            src_ref=given.at[0, place],
+            dst_ref=landing.at[place],
+            send_sem=sum_send.at[place],
+            recv_sem=arrived.at[place],
+            device_id=(section, up if going_up else down),
             device_id_type=MESH,
         )
 
@@ -406,102 +549,196 @@
         falling = jnp.logical_and(middle, lax.rem(m, 2) == 1)
         home = lax.rem(jnp.where(falling, z - away, z + away) + N_Z, N_Z)
         block = PER_Z * home + which
-        odd = lax.rem(block, 2)
+        odd = more_down(home, which)
         mine = core_of(block) == core
+        across = by_y(home, which)
+        mine_give = jnp.logical_and(mine, across)
+        mine_relay = jnp.logical_and(mine_give, lax.div(which, 3) == my_y)
+        mine_ring = jnp.logical_and(mine, jnp.logical_not(across))
         rises = jnp.where(middle, jnp.logical_not(falling), odd == 0)
         has_low = jnp.logical_or(last, jnp.logical_and(rises, away < 4 - odd))
         has_high = jnp.logical_or(last, jnp.logical_and(jnp.logical_not(rises), away < 3 + odd))
-        go_up = jnp.logical_and(mine, jnp.logical_and(rises, jnp.logical_not(last)))
-        go_down = jnp.logical_and(mine, jnp.logical_and(jnp.logical_not(rises), jnp.logical_not(last)))
-        return place_of(block), which, mine, has_low, has_high, go_up, go_down, jnp.logical_and(mine, last)
-
-    def reduce(n, carry):
-        place, which, mine, has_low, has_high, go_up, go_down, last = sum_step(n)
-
-        @pl.when(mine)
-        def _():
-            rows = pl.ds(pl.multiple_of(place * CHUNK, CHUNK), CHUNK)
-            side = jnp.where(place >= QKV_BLOCKS, 1, 0)
-            for tile in range(4):
-                columns = slice(tile * width // 4, (tile + 1) * width // 4)
-                value = nn(lhs[0, rows, :], acts[side, 0, :, columns])
-                for batch in range(1, 2 * MB):
-                    value = value + nn(lhs[batch, rows, :], acts[side, batch, :, columns])
-                total[:, columns] = value
-
-        @pl.when(jnp.logical_and(mine, has_low))
+        go_up = jnp.logical_and(rises, jnp.logical_not(last))
+        go_down = jnp.logical_and(jnp.logical_not(rises), jnp.logical_not(last))
+        return place_of(block), which, mine_ring, mine_give, mine_relay, has_low, has_high, go_up, go_down, last
+
+    def block_gradient(place):
+        rows = pl.ds(pl.multiple_of(place * CHUNK, CHUNK), CHUNK)
+        side = jnp.where(place >= QKV_BLOCKS, 1, 0)
+        for tile in range(4):
+            columns = slice(tile * width // 4, (tile + 1) * width // 4)
+            value = nn(lhs[0, rows, :], acts[side, 0, :, columns])
+            for batch in range(1, 2 * MB):
+                value = value + nn(lhs[batch, rows, :], acts[side, batch, :, columns])
+            total[:, columns] = value
+
+    def give(n):
+        place, which, _, mine_give, _, _, _, _, _, _ = sum_step(n)
+
+        @pl.when(mine_give)
+        def _():
+            block_gradient(place)
+            stage[place] = total[...].astype(BF16)
+            give_copy(place, which).start()
+
+    def reduce(n):
+        place, which, mine_ring, _, mine_relay, has_low, has_high, go_up, go_down, last = sum_step(n)
+
+        @pl.when(mine_ring)
+        def _():
+            block_gradient(place)
+
+        @pl.when(mine_relay)
+        def _():
+            for source in range(2):
+                pltpu.make_async_remote_copy(
+                    src_ref=given.at[source, place],
+                    dst_ref=given.at[source, place],
+                    send_sem=give_send.at[place],
+                    recv_sem=give_recv.at[LOCAL * source + place],
+                    device_id=(partner, dp),
+                    device_id_type=MESH,
+                ).wait_recv()
+            total[...] = given[0, place].astype(F32) + given[1, place].astype(F32)
+
+        active = jnp.logical_or(mine_ring, mine_relay)
+
+        @pl.when(jnp.logical_and(active, has_low))
         def _():
             sum_copy(place, True).wait_recv()
             total[...] += from_low[place].astype(F32)
 
-        @pl.when(jnp.logical_and(mine, has_high))
+        @pl.when(jnp.logical_and(active, has_high))
         def _():
             sum_copy(place, False).wait_recv()
             total[...] += from_high[place].astype(F32)
 
-        @pl.when(mine)
+        @pl.when(mine_ring)
         def _():
             stage[place] = total[...].astype(BF16)
 
-        @pl.when(go_up)
-        def _():
-            sum_copy(place, True).start()
-
-        @pl.when(go_down)
-        def _():
-            sum_copy(place, False).start()
-
-        @pl.when(last)
+        @pl.when(mine_relay)
+        def _():
+            given[0, place] = total[...].astype(BF16)
+
+        for going_up, goes in ((True, go_up), (False, go_down)):
+
+            @pl.when(jnp.logical_and(mine_ring, goes))
+            def _(going_up=going_up):
+                sum_copy(place, going_up).start()
+
+            @pl.when(jnp.logical_and(mine_relay, goes))
+            def _(going_up=going_up):
+                relay_sum_copy(place, going_up).start()
+
+        @pl.when(jnp.logical_and(mine_ring, last))
         def _():
             for quarter in range(CHUNK // PIECE):
                 final_copy(which, quarter).start()
 
+        for quarter in range(CHUNK // PIECE):
+            keeper, _ = keeper_of(which, quarter)
+            here = lax.rem(keeper, 2) == core
+
+            @pl.when(jnp.logical_and(jnp.logical_and(mine_relay, last), here))
+            def _(quarter=quarter):
+                relay_final(which, quarter, True).start()
+
+            @pl.when(jnp.logical_and(jnp.logical_and(mine_relay, last), jnp.logical_not(here)))
+            def _(quarter=quarter):
+                relay_final(which, quarter, False).start()
+
+    def lead(n, carry):
+        give(n)
         return carry
 
-    lax.fori_loop(0, 40, reduce, 0)
-
-    for copy in id_copies + pick_copies + norm_copies + pass_copies:
+    def both(n, carry):
+        @pl.when(n < 40)
+        def _():
+            give(n)
+
+        reduce(n - LEAD)
+        return carry
+
+    lax.fori_loop(0, LEAD, lead, 0)
+    lax.fori_loop(LEAD, 40 + LEAD, both, 0)
+
+    for copy in id_copies + pick_copies + own_copies + pass_copies:
         copy.wait_send()
     for piece in range(PIECES):
-        for half_y in range(2):
-            first_copy(piece, half_y).wait_send()
+        across, _, there = piece_way(piece)
+
+        @pl.when(jnp.logical_not(across))
+        def _(piece=piece):
+            for half_y in range(2):
+                first_copy(piece, half_y).wait_send()
+
+        @pl.when(there)
+        def _(piece=piece):
+            relay_piece(piece, False).wait_send()
 
     def drain(n, carry):
-        place, _, send_up, send_down = gather_step(n)
-
-        @pl.when(send_up)
-        def _():
-            gather_copy(place, True).wait_send()
-
-        @pl.when(send_down)
-        def _():
-            gather_copy(place, False).wait_send()
-
-        place, which, _, _, _, go_up, go_down, last = sum_step(n)
-
-        @pl.when(jnp.logical_or(go_up, go_down))
+        place, mine_ring, mine_relay, send_up, send_down = gather_step(n)
+        for going_up, goes in ((True, send_up), (False, send_down)):
+
+            @pl.when(jnp.logical_and(mine_ring, goes))
+            def _(going_up=going_up):
+                gather_copy(place, going_up).wait_send()
+
+            @pl.when(jnp.logical_and(mine_relay, goes))
+            def _(going_up=going_up):
+                relay_copy(place, going_up).wait_send()
+
+        @pl.when(mine_relay)
+        def _():
+            for half_y in range(2):
+                relay_over(place, half_y).wait_send()
+
+        place, which, mine_ring, mine_give, mine_relay, _, _, _, _, last = sum_step(n)
+        active = jnp.logical_or(mine_ring, mine_relay)
+
+        @pl.when(jnp.logical_and(active, jnp.logical_not(last)))
         def _():
             sum_copy(place, True).wait_send()
 
-        @pl.when(last)
-        def _():
-            for quarter in range(CHUNK // PIECE):
+        @pl.when(mine_give)
+        def _():
+            give_copy(place, which).wait_send()
+
+        for quarter in range(CHUNK // PIECE):
+            keeper, _ = keeper_of(which, quarter)
+            away_core = lax.rem(keeper, 2) != core
+            sent_on = jnp.logical_or(mine_ring, jnp.logical_and(mine_relay, away_core))
+
+            @pl.when(jnp.logical_and(last, sent_on))
+            def _(quarter=quarter):
                 final_copy(which, quarter).wait_send()
 
         return carry
 
     lax.fori_loop(0, 40, drain, 0)
 
-    for source in range(2):
+    def final_wait(piece, source):
+        rows = pl.ds(PIECE * piece, PIECE)
         pltpu.make_async_remote_copy(
-            src_ref=final.at[source],
-            dst_ref=final.at[source],
+            src_ref=final.at[source, rows],
+            dst_ref=final.at[source, rows],
             send_sem=final_send.at[0],
-            recv_sem=final_recv.at[source],
-            device_id=(after, dp),
+            recv_sem=final_recv.at[PIECES * source + piece],
+            device_id=(section, sibling),
             device_id_type=MESH,
         ).wait_recv()
-    grad_ref[...] = final[0].astype(F32) + final[1].astype(F32)
+
+    for piece in range(PIECES):
+        rows = pl.ds(PIECE * piece, PIECE)
+        across, _, _ = piece_way(piece)
+        final_wait(piece, 0)
+        grad_ref[rows, :] = final[0, rows, :].astype(F32)
+
+        @pl.when(jnp.logical_not(across))
+        def _(piece=piece, rows=rows):
+            final_wait(piece, 1)
+            grad_ref[rows, :] += final[1, rows, :].astype(F32)
 
 
 def summed_gradient(params, sent, back, ids):
@@ -529,13 +766,15 @@
             pltpu.SMEM((8, 128), jnp.int32),
             pltpu.SMEM((8, 128), jnp.int32),
             pltpu.VMEM((LOCAL, CHUNK, width), BF16),
+            pltpu.VMEM((LOCAL, CHUNK, width), BF16),
             pltpu.VMEM((2, 2 * MB, SEQ, width), BF16),
-            pltpu.VMEM((MB, SEQ, width), BF16),
+            pltpu.VMEM((2, MB, SEQ, width), BF16),
             pltpu.VMEM((2 * MB, O_AT, SEQ), F32),
             pltpu.VMEM((2 * MB, Q_ROWS, SEQ), BF16),
             pltpu.VMEM((2 * MB, LOCAL * CHUNK, SEQ), BF16),
             pltpu.VMEM((CHUNK, width), F32),
             pltpu.VMEM((LOCAL, CHUNK, width), BF16),
+            pltpu.VMEM((2, LOCAL, CHUNK, width), BF16),
             pltpu.VMEM((LOCAL, CHUNK, width), BF16),
             pltpu.VMEM((LOCAL, CHUNK, width), BF16),
             pltpu.VMEM((2, SHARD, width), BF16),
@@ -547,17 +786,24 @@
             dma((LOCAL,)),
             dma((LOCAL,)),
             dma((LOCAL,)),
+            dma((LOCAL,)),
+            dma((LOCAL,)),
+            dma((2 * LOCAL,)),
+            dma((LOCAL,)),
             dma((MB,)),
             dma((MB,)),
             dma((MB,)),
             dma((MB,)),
             dma((MB,)),
             dma((MB,)),
-            dma((LOCAL,)),
-            dma((LOCAL,)),
-            dma((LOCAL,)),
+            dma((MB,)),
+            dma((LOCAL,)),
+            dma((LOCAL,)),
+            dma((LOCAL,)),
+            dma((LOCAL,)),
+            dma((2 * LOCAL,)),
             dma((4 * PER_Z,)),
-            dma((2,)),
+            dma((2 * PIECES,)),
         ],
         compiler_params=pltpu.CompilerParams(
             collective_id=0, has_side_effects=True, vmem_limit_bytes=60 * 1024 * 1024

time: 172 us -> 156 us (0.907)
  the two profiles are of different devices: /device:TPU:48 before, /device:TPU:24 now
where the time goes in v2:
time: 156 us
  Pallas kernels  152 us (97%)
  other arithmetic  2.78 us (2%)
    pallas_call x1, Pallas kernels, summed_gradient(): pl.pallas_call(kernel, out_shape=jax.ShapeDtypeStruct((SHARD, width), F32...  152 us

profile of v2, /device:TPU:24, one launch (start us, length us, event | category | flops | bytes accessed | tf_op | source)
XLA Modules:
  0.0 156.3 jit_solution(8969499462491414669)
XLA Ops:
  0.6 0.7 concatenate.5
  1.3 0.7 concatenate.6.ids_ref
  2.0 0.0 copy-start
  2.0 0.0 copy-start.1
  2.0 0.0 copy-start.2
  2.0 151.5 %shard_map.103 = f32[80,2048]{1,0:T(8,128)} custom-call(bf16[80,2048]{1,0:T(8,128)(2,1)} %bitcast.25, bf16[4,192,2048]{2,1,0:T(8,128)(2,1)} %bitcast.23, bf16[4,192,2048]{2,1,0:T(8,128)(2,1)} %bitcast.24, s32[8,128]{1,0:T(8,128)} %concatenate.6.ids_ref, f32[32,192]{1,0:T(8,128)} %constant.30.clone.cos_ref, f32[32,192]{1,0:T(8,128)} %constant.31.clone.sin_ref), custom_call_target="tpu_custom_call" | custom-call | tf_op jit(solution)/shard_map/pallas_call | solution.py:755
  153.5 0.0 copy-done
  153.5 0.0 copy-done.1
  153.5 0.0 copy-done.2
  153.5 2.8 %fusion.5 = (f32[1,80,2048]{2,1,0:T(8,128)}, bf16[1,80,2048]{2,1,0:T(8,128)(2,1)}, f32[1,80,2048]{2,1,0:T(8,128)}) fusion(f32[80,2048]{1,0:T(8,128)} %shard_map.103, f32[1,80,2048]{2,1,0:T(8,128)S(1)} %copy-done.1, f32[1,80,2048]{2,1,0:T(8,128)S(1)} %copy-done.2, bf16[1,80,2048]{2,1,0:T(8,128)(2,1)S(1)} %copy-done), kind=kLoop, calls=%fused_computation.9 | loop fusion | flops 2949120 | bytes 3932160 | tf_op jit(solution)/shard_map/broadcast_in_dim | solution.py:828
Async XLA Ops:
  2.0 151.5 %copy-start = (bf16[1,80,2048]{2,1,0:T(8,128)(2,1)S(1)}, bf16[1,80,2048]{2,1,0:T(8,128)(2,1)}, u32[]{:S(2)}) copy-start(bf16[1,80,2048]{2,1,0:T(8,128)(2,1)} %param.8) | copy-start | bytes 983044
  2.0 151.5 %copy-start.1 = (f32[1,80,2048]{2,1,0:T(8,128)S(1)}, f32[1,80,2048]{2,1,0:T(8,128)}, u32[]{:S(2)}) copy-start(f32[1,80,2048]{2,1,0:T(8,128)} %param.10) | copy-start | bytes 1966084
  2.0 151.5 %copy-start.2 = (f32[1,80,2048]{2,1,0:T(8,128)S(1)}, f32[1,80,2048]{2,1,0:T(8,128)}, u32[]{:S(2)}) copy-start(f32[1,80,2048]{2,1,0:T(8,128)} %param.9) | copy-start | bytes 1966084

commit v3 on v2

--- a/solution.py
+++ b/solution.py
@@ -22,7 +22,7 @@
 PER_Z = 5
 LOCAL = 20
 SHARD = 80
-LEAD = 8
+LEAD = 12
 PIECE = 16
 PIECES = SHARD // PIECE
 Q_ROWS = 512
@@ -72,6 +72,14 @@
     even = lax.rem(home, 2) == 0
     stays = jnp.logical_or(which == 2, which == jnp.where(even, 0, 4))
     return jnp.logical_not(stays)
+
+
+def in_order(home, turn, ring_first):
+    even = lax.rem(home, 2) == 0
+    turn = jnp.where(ring_first, lax.rem(turn + 3, PER_Z), turn)
+    of_even = jnp.where(turn < 2, 2 * turn + 1, jnp.where(turn == 2, 4, 2 * turn - 6))
+    of_odd = jnp.where(turn < 2, turn, jnp.where(turn == 2, 3, 2 * turn - 4))
+    return jnp.where(even, of_even, of_odd)
 
 
 def more_down(home, which):
@@ -331,9 +339,10 @@
         m = n - PER_Z
         middle = jnp.logical_and(n >= PER_Z, n < 35)
         away = jnp.where(n < PER_Z, 0, jnp.where(middle, 1 + lax.div(m, 10), 4))
-        which = jnp.where(n < PER_Z, n, jnp.where(middle, lax.div(lax.rem(m, 10), 2), n - 35))
+        turn = jnp.where(n < PER_Z, n, jnp.where(middle, lax.div(lax.rem(m, 10), 2), n - 35))
         rising = jnp.logical_and(middle, lax.rem(m, 2) == 0)
         home = lax.rem(jnp.where(rising, z - away, z + away) + N_Z, N_Z)
+        which = in_order(home, turn, False)
         block = PER_Z * home + which
         odd = more_down(home, which)
         mine = core_of(block) == core
@@ -545,9 +554,10 @@
         middle = jnp.logical_and(n >= PER_Z, n < 35)
         last = n >= 35
         away = jnp.where(n < PER_Z, 4, jnp.where(middle, 3 - lax.div(m, 10), 0))
-        which = jnp.where(n < PER_Z, n, jnp.where(middle, lax.div(lax.rem(m, 10), 2), n - 35))
+        turn = jnp.where(n < PER_Z, n, jnp.where(middle, lax.div(lax.rem(m, 10), 2), n - 35))
         falling = jnp.logical_and(middle, lax.rem(m, 2) == 1)
         home = lax.rem(jnp.where(falling, z - away, z + away) + N_Z, N_Z)
+        which = in_order(home, turn, True)
         block = PER_Z * home + which
         odd = more_down(home, which)
         mine = core_of(block) == core

time: 156 us -> 149 us (0.955)
  the two profiles are of different devices: /device:TPU:24 before, /device:TPU:6 now
where the time goes in v3:
time: 149 us
  Pallas kernels  144 us (97%)
  other arithmetic  2.78 us (2%)
    pallas_call x1, Pallas kernels, summed_gradient(): pl.pallas_call(kernel, out_shape=jax.ShapeDtypeStruct((SHARD, width), F32...  144 us

profile of v3, /device:TPU:6, one launch (start us, length us, event | category | flops | bytes accessed | tf_op | source)
XLA Modules:
  0.0 149.0 jit_solution(17590239974654921361)
XLA Ops:
  0.6 0.7 concatenate.5
  1.3 0.7 concatenate.6.ids_ref
  2.0 0.0 copy-start
  2.0 0.0 copy-start.1
  2.0 0.0 copy-start.2
  2.0 144.2 %shard_map.103 = f32[80,2048]{1,0:T(8,128)} custom-call(bf16[80,2048]{1,0:T(8,128)(2,1)} %bitcast.25, bf16[4,192,2048]{2,1,0:T(8,128)(2,1)} %bitcast.23, bf16[4,192,2048]{2,1,0:T(8,128)(2,1)} %bitcast.24, s32[8,128]{1,0:T(8,128)} %concatenate.6.ids_ref, f32[32,192]{1,0:T(8,128)} %constant.30.clone.cos_ref, f32[32,192]{1,0:T(8,128)} %constant.31.clone.sin_ref), custom_call_target="tpu_custom_call" | custom-call | tf_op jit(solution)/shard_map/pallas_call | solution.py:765
  146.2 0.0 copy-done
  146.2 0.0 copy-done.1
  146.2 0.0 copy-done.2
  146.2 2.8 %fusion.5 = (f32[1,80,2048]{2,1,0:T(8,128)}, bf16[1,80,2048]{2,1,0:T(8,128)(2,1)}, f32[1,80,2048]{2,1,0:T(8,128)}) fusion(f32[80,2048]{1,0:T(8,128)} %shard_map.103, f32[1,80,2048]{2,1,0:T(8,128)S(1)} %copy-done.1, f32[1,80,2048]{2,1,0:T(8,128)S(1)} %copy-done.2, bf16[1,80,2048]{2,1,0:T(8,128)(2,1)S(1)} %copy-done), kind=kLoop, calls=%fused_computation.9 | loop fusion | flops 2949120 | bytes 3932160 | tf_op jit(solution)/shard_map/broadcast_in_dim | solution.py:838
Async XLA Ops:
  2.0 144.2 %copy-start = (bf16[1,80,2048]{2,1,0:T(8,128)(2,1)S(1)}, bf16[1,80,2048]{2,1,0:T(8,128)(2,1)}, u32[]{:S(2)}) copy-start(bf16[1,80,2048]{2,1,0:T(8,128)(2,1)} %param.8) | copy-start | bytes 983044
  2.0 144.2 %copy-start.1 = (f32[1,80,2048]{2,1,0:T(8,128)S(1)}, f32[1,80,2048]{2,1,0:T(8,128)}, u32[]{:S(2)}) copy-start(f32[1,80,2048]{2,1,0:T(8,128)} %param.10) | copy-start | bytes 1966084
  2.0 144.2 %copy-start.2 = (f32[1,80,2048]{2,1,0:T(8,128)S(1)}, f32[1,80,2048]{2,1,0:T(8,128)}, u32[]{:S(2)}) copy-start(f32[1,80,2048]{2,1,0:T(8,128)} %param.9) | copy-start | bytes 1966084

commit v4 on v3

--- a/solution.py
+++ b/solution.py
@@ -23,6 +23,7 @@
 LOCAL = 20
 SHARD = 80
 LEAD = 12
+STACK = 4
 PIECE = 16
 PIECES = SHARD // PIECE
 Q_ROWS = 512
@@ -251,60 +252,6 @@
         def _(piece=piece):
             relay_piece(piece, False).start()
 
-    stays, leaves = odd_section, 1 - odd_section
-    target_section = jnp.where(odd_section == 0, before_two, after_two)
-    id_copies[0].wait_recv()
-    to_one = pltpu.make_async_copy(ids_next, ids_one, sem_ids.at[0])
-    to_one.start()
-    to_one.wait()
-    id_copies[1].wait_recv()
-    to_two = pltpu.make_async_copy(ids_prev, ids_two, sem_ids.at[1])
-    to_two.start()
-    to_two.wait()
-    loads[1].wait()
-    loads[2].wait()
-    own_copies = []
-    own_locals = []
-    pick_copies = []
-    for m in range(MB):
-        wanted_one, wanted_two = ids_one[m, 0], ids_two[m, 0]
-
-        def pick_rows(n, carry, m=m, wanted_one=wanted_one, wanted_two=wanted_two):
-            rows = pl.ds(pl.multiple_of(n * 16, 16), 16)
-            value = sent[wanted_one, rows, :].astype(F32)
-            scaling = lax.rsqrt(jnp.mean(value * value, axis=-1, keepdims=True) + 1e-05)
-            picked[0, m, rows, :] = (value * scaling).astype(BF16)
-            picked[1, m, rows, :] = back[wanted_two, rows, :]
-            return carry
-
-        lax.fori_loop(0, SEQ // 16, pick_rows, 0)
-        pick_copies.append(
-            pltpu.make_async_remote_copy(
-                src_ref=picked.at[leaves, m],
-                dst_ref=acts.at[leaves, 2 * core + m],
-                send_sem=pick_send.at[m],
-                recv_sem=pick_recv.at[m],
-                device_id=(target_section, dp),
-                device_id_type=MESH,
-            )
-        )
-        own_copies.append(
-            pltpu.make_async_remote_copy(
-                src_ref=picked.at[stays, m],
-                dst_ref=acts.at[stays, 2 * core + m],
-                send_sem=own_send.at[m],
-                recv_sem=own_recv.at[m],
-                device_id=(section, sibling),
-                device_id_type=MESH,
-            )
-        )
-        own_locals.append(
-            pltpu.make_async_copy(picked.at[stays, m], acts.at[stays, 2 * core + m], own_local.at[m])
-        )
-        pick_copies[m].start()
-        own_copies[m].start()
-        own_locals[m].start()
-
     def gather_copy(place, going_up):
         return pltpu.make_async_remote_copy(
             src_ref=weights.at[place],
@@ -389,7 +336,63 @@
 
         return carry
 
-    lax.fori_loop(0, 40, gather, 0)
+    lax.fori_loop(0, 3, gather, 0)
+
+    stays, leaves = odd_section, 1 - odd_section
+    target_section = jnp.where(odd_section == 0, before_two, after_two)
+    id_copies[0].wait_recv()
+    to_one = pltpu.make_async_copy(ids_next, ids_one, sem_ids.at[0])
+    to_one.start()
+    to_one.wait()
+    id_copies[1].wait_recv()
+    to_two = pltpu.make_async_copy(ids_prev, ids_two, sem_ids.at[1])
+    to_two.start()
+    to_two.wait()
+    loads[1].wait()
+    loads[2].wait()
+    own_copies = []
+    own_locals = []
+    pick_copies = []
+    for m in range(MB):
+        wanted_one, wanted_two = ids_one[m, 0], ids_two[m, 0]
+
+        def pick_rows(n, carry, m=m, wanted_one=wanted_one, wanted_two=wanted_two):
+            rows = pl.ds(pl.multiple_of(n * 16, 16), 16)
+            value = sent[wanted_one, rows, :].astype(F32)
+            scaling = lax.rsqrt(jnp.mean(value * value, axis=-1, keepdims=True) + 1e-05)
+            picked[0, m, rows, :] = (value * scaling).astype(BF16)
+            picked[1, m, rows, :] = back[wanted_two, rows, :]
+            return carry
+
+        lax.fori_loop(0, SEQ // 16, pick_rows, 0)
+        pick_copies.append(
+            pltpu.make_async_remote_copy(
+                src_ref=picked.at[leaves, m],
+                dst_ref=acts.at[leaves, 2 * core + m],
+                send_sem=pick_send.at[m],
+                recv_sem=pick_recv.at[m],
+                device_id=(target_section, dp),
+                device_id_type=MESH,
+            )
+        )
+        own_copies.append(
+            pltpu.make_async_remote_copy(
+                src_ref=picked.at[stays, m],
+                dst_ref=acts.at[stays, 2 * core + m],
+                send_sem=own_send.at[m],
+                recv_sem=own_recv.at[m],
+                device_id=(section, sibling),
+                device_id_type=MESH,
+            )
+        )
+        own_locals.append(
+            pltpu.make_async_copy(picked.at[stays, m], acts.at[stays, 2 * core + m], own_local.at[m])
+        )
+        pick_copies[m].start()
+        own_copies[m].start()
+        own_locals[m].start()
+
+    lax.fori_loop(3, 40, gather, 0)
 
     pass_copies = []
     for m in range(MB):
@@ -422,21 +425,19 @@
         own_copies[m].wait_recv()
         pass_copies[m].wait_recv()
 
-    def project(n, carry):
-        batch, part = lax.div(n, 3), lax.rem(n, 3)
-        rows = weights[pl.ds(4 * part, 4)].reshape(4 * CHUNK, width)
-        proj[batch, pl.ds(pl.multiple_of(part * 256, 256), 256), :] = nt(rows, acts[0, batch])
+    def project(batch, carry):
+        rows = weights[:QKV_BLOCKS].reshape(O_AT, width)
+        proj[batch] = nt(rows, acts[0, batch])
         return carry
 
-    lax.fori_loop(0, 12, project, 0)
-
-    def cotangent(n, carry):
-        batch, part = lax.div(n, 2), lax.rem(n, 2)
-        rows = weights[pl.ds(QKV_BLOCKS + 4 * part, 4)].reshape(4 * CHUNK, width)
-        dctx[batch, pl.ds(pl.multiple_of(part * 256, 256), 256), :] = nt(rows, acts[1, batch]).astype(BF16)
+    lax.fori_loop(0, 2 * MB, project, 0)
+
+    def cotangent(batch, carry):
+        rows = weights[QKV_BLOCKS:].reshape(Q_ROWS, width)
+        dctx[batch] = nt(rows, acts[1, batch]).astype(BF16)
         return carry
 
-    lax.fori_loop(0, 8, cotangent, 0)
+    lax.fori_loop(0, 2 * MB, cotangent, 0)
 
     cosine, sine = cos_ref[...], sin_ref[...]
     half = HEAD_SIZE // 2
@@ -459,27 +460,35 @@
         value = value_t.T.astype(BF16)
         key_t = key_t.astype(BF16)
         value_t = value_t.astype(BF16)
+        ones = jnp.ones((16, SEQ), BF16)
+        value_ones = jnp.concatenate([value_t, ones], axis=0)
         kept = lax.broadcasted_iota(jnp.int32, (SEQ, SEQ), 0) <= lax.broadcasted_iota(jnp.int32, (SEQ, SEQ), 1)
+        kept = jnp.concatenate([kept.astype(jnp.int32)] * STACK, axis=1) > 0
         dkey = jnp.zeros((HEAD_SIZE, SEQ), F32)
         dvalue = jnp.zeros((HEAD_SIZE, SEQ), F32)
-        for head in range(4):
-            first = 256 * group + HEAD_SIZE * head
-            rows = pl.ds(pl.multiple_of(first, HEAD_SIZE), HEAD_SIZE)
-            query_t = (rotate(proj[batch, rows, :]) * HEAD_SIZE**-0.5).astype(BF16)
+        for stack in range(4 // STACK):
+            firsts = [256 * group + HEAD_SIZE * (STACK * stack + head) for head in range(STACK)]
+            rows = [pl.ds(pl.multiple_of(first, HEAD_SIZE), HEAD_SIZE) for first in firsts]
+            query_t = [(rotate(proj[batch, row, :]) * HEAD_SIZE**-0.5) for row in rows]
+            query_t = jnp.concatenate(query_t, axis=1).astype(BF16)
             scores = jnp.where(kept, nn(key, query_t), -1e30)
             raised = jnp.exp(scores - jnp.max(scores, axis=0, keepdims=True))
-            probs = raised * (1.0 / jnp.sum(raised, axis=0, keepdims=True))
-            probs_b = probs.astype(BF16)
-            context_rows = pl.ds(pl.multiple_of(O_AT + first, HEAD_SIZE), HEAD_SIZE)
-            lhs[batch, context_rows, :] = nn(value_t, probs_b).astype(BF16)
-            cot = dctx[batch, rows, :]
-            dprobs = nn(value, cot)
-            dvalue = dvalue + nt(cot, probs_b)
-            delta = jnp.sum(dprobs * probs, axis=0, keepdims=True)
-            dscores = (probs * (dprobs - delta)).astype(BF16)
+            raised_b = raised.astype(BF16)
+            context = nn(value_ones, raised_b)
+            inverse = 1.0 / context[HEAD_SIZE : HEAD_SIZE + 1]
+            context = context[:HEAD_SIZE] * inverse
+            cot = jnp.concatenate([dctx[batch, row, :].astype(F32) for row in rows], axis=1)
+            delta = jnp.sum(cot * context, axis=0, keepdims=True) * inverse
+            cot = (cot * inverse).astype(BF16)
+            dscores = (raised * (nn(value, cot) - delta)).astype(BF16)
+            dvalue = dvalue + nt(cot, raised_b)
             dquery = nn(key_t, dscores) * HEAD_SIZE**-0.5
-            lhs[batch, rows, :] = rotate_back(dquery).astype(BF16)
             dkey = dkey + nt(query_t, dscores)
+            for head in range(STACK):
+                lanes = slice(SEQ * head, SEQ * (head + 1))
+                context_rows = pl.ds(pl.multiple_of(O_AT + firsts[head], HEAD_SIZE), HEAD_SIZE)
+                lhs[batch, context_rows, :] = context[:, lanes].astype(BF16)
+                lhs[batch, rows[head], :] = rotate_back(dquery[:, lanes]).astype(BF16)
         lhs[batch, key_rows, :] = rotate_back(dkey).astype(BF16)
         lhs[batch, value_rows, :] = dvalue.astype(BF16)
         return carry
@@ -757,8 +766,7 @@
     angles = frequency[:, None] * np.arange(SEQ, dtype=np.float64)[None, :]
     cosine = jnp.asarray(np.cos(angles), F32)
     sine = jnp.asarray(np.sin(angles), F32)
-    wide_ids = jnp.broadcast_to(ids.reshape(MB, 1), (MB, 128))
-    wide_ids = jnp.concatenate([wide_ids, jnp.zeros((8 - MB, 128), jnp.int32)], axis=0)
+    wide_ids = jnp.broadcast_to(ids.reshape(1, MB, 1), (4, MB, 128)).reshape(8, 128)
     dma = pltpu.SemaphoreType.DMA
     in_vmem = pl.BlockSpec(memory_space=pltpu.VMEM)
     anywhere = pl.BlockSpec(memory_space=pl.ANY)

time: 149 us -> 135 us (0.906)
  Pallas kernels: 144 us -> 130 us
    pallas_call x1, Pallas kernels: 144 us -> 130 us  [summed_gradient(): pl.pallas_call(kernel, out_shape=jax.ShapeDtypeStruct((SHARD, width), F32...]
where the time goes in v4:
time: 135 us; the launch traced here: 134 us
  Pallas kernels  130 us (96%)
  other arithmetic  2.78 us (2%)
  local copies, waits for them, and re-layouts  1.42 us (1%)
    pallas_call x1, Pallas kernels, summed_gradient(): pl.pallas_call(kernel, out_shape=jax.ShapeDtypeStruct((SHARD, width), F32...  130 us
    broadcast_in_dim x1, other arithmetic, shards(): return (renewed[None], first_new[None], second_new[None])  2.78 us

profile of v4, /device:TPU:6, one launch (start us, length us, event | category | flops | bytes accessed | tf_op | source)
XLA Modules:
  0.0 134.5 jit_solution(18309882474535912649)
XLA Ops:
  0.6 0.7 broadcast_in_dim.21
  1.3 0.1 broadcast_in_dim.22
  1.4 0.7 broadcast_in_dim.23.ids_ref
  2.0 0.0 copy-start
  2.0 0.0 copy-start.1
  2.0 0.0 copy-start.2
  2.0 129.6 %shard_map.103 = f32[80,2048]{1,0:T(8,128)} custom-call(bf16[80,2048]{1,0:T(8,128)(2,1)} %bitcast.25, bf16[4,192,2048]{2,1,0:T(8,128)(2,1)} %bitcast.23, bf16[4,192,2048]{2,1,0:T(8,128)(2,1)} %bitcast.24, s32[8,128]{1,0:T(8,128)} %broadcast_in_dim.23.ids_ref, f32[32,192]{1,0:T(8,128)} %constant.28.clone.cos_ref, f32[32,192]{1,0:T(8,128)} %constant.29.clone.sin_ref), custom_call_target="tpu_custom_call" | custom-call | tf_op jit(solution)/shard_map/pallas_call | solution.py:773
  131.7 0.0 copy-done
  131.7 0.0 copy-done.1
  131.7 0.0 copy-done.2
  131.7 2.8 %fusion.5 = (f32[1,80,2048]{2,1,0:T(8,128)}, bf16[1,80,2048]{2,1,0:T(8,128)(2,1)}, f32[1,80,2048]{2,1,0:T(8,128)}) fusion(f32[80,2048]{1,0:T(8,128)} %shard_map.103, f32[1,80,2048]{2,1,0:T(8,128)S(1)} %copy-done.1, f32[1,80,2048]{2,1,0:T(8,128)S(1)} %copy-done.2, bf16[1,80,2048]{2,1,0:T(8,128)(2,1)S(1)} %copy-done), kind=kLoop, calls=%fused_computation.9 | loop fusion | flops 2949120 | bytes 3932160 | tf_op jit(solution)/shard_map/broadcast_in_dim | solution.py:846
Async XLA Ops:
  2.0 129.6 %copy-start = (bf16[1,80,2048]{2,1,0:T(8,128)(2,1)S(1)}, bf16[1,80,2048]{2,1,0:T(8,128)(2,1)}, u32[]{:S(2)}) copy-start(bf16[1,80,2048]{2,1,0:T(8,128)(2,1)} %param.8) | copy-start | bytes 983044
  2.0 129.6 %copy-start.1 = (f32[1,80,2048]{2,1,0:T(8,128)S(1)}, f32[1,80,2048]{2,1,0:T(8,128)}, u32[]{:S(2)}) copy-start(f32[1,80,2048]{2,1,0:T(8,128)} %param.10) | copy-start | bytes 1966084
  2.0 129.6 %copy-start.2 = (f32[1,80,2048]{2,1,0:T(8,128)S(1)}, f32[1,80,2048]{2,1,0:T(8,128)}, u32[]{:S(2)}) copy-start(f32[1,80,2048]{2,1,0:T(8,128)} %param.9) | copy-start | bytes 1966084

commit v5 on v4

--- a/solution.py
+++ b/solution.py
@@ -24,6 +24,8 @@
 SHARD = 80
 LEAD = 12
 STACK = 4
+PARTS = 1
+PART = CHUNK // PARTS
 PIECE = 16
 PIECES = SHARD // PIECE
 Q_ROWS = 512
@@ -49,45 +51,61 @@
     return lax.dot_general(a, b, (((1,), (1,)), ((), ())), preferred_element_type=F32)
 
 
+def half(value):
+    return lax.shift_right_logical(value, 1)
+
+
+def low_bit(value):
+    return lax.bitwise_and(value, 1)
+
+
+def round_z(value):
+    return lax.bitwise_and(value + N_Z, N_Z - 1)
+
+
 def core_of(block):
     return jnp.where(
         block < 16,
-        lax.div(block, 8),
-        jnp.where(block < 24, lax.rem(lax.div(block - 16, 2), 2), lax.div(block - 24, 8)),
+        jnp.where(block < 8, 0, 1),
+        jnp.where(block < 24, low_bit(half(block)), jnp.where(block < 32, 0, 1)),
     )
 
 
 def place_of(block):
     return jnp.where(
         block < 16,
-        lax.rem(block, 8),
+        lax.bitwise_and(block, 7),
         jnp.where(
             block < 24,
-            8 + 2 * lax.div(block - 16, 4) + lax.rem(block - 16, 2),
-            12 + lax.rem(block - 24, 8),
+            jnp.where(block < 20, 8, 10) + low_bit(block),
+            12 + lax.bitwise_and(block, 7),
         ),
     )
 
 
+def tens(value):
+    return jnp.where(value < 10, 0, jnp.where(value < 20, 1, 2))
+
+
 def by_y(home, which):
-    even = lax.rem(home, 2) == 0
+    even = low_bit(home) == 0
     stays = jnp.logical_or(which == 2, which == jnp.where(even, 0, 4))
     return jnp.logical_not(stays)
 
 
 def in_order(home, turn, ring_first):
-    even = lax.rem(home, 2) == 0
-    turn = jnp.where(ring_first, lax.rem(turn + 3, PER_Z), turn)
+    even = low_bit(home) == 0
+    turn = jnp.where(ring_first, jnp.where(turn < 2, turn + 3, turn - 2), turn)
     of_even = jnp.where(turn < 2, 2 * turn + 1, jnp.where(turn == 2, 4, 2 * turn - 6))
     of_odd = jnp.where(turn < 2, turn, jnp.where(turn == 2, 3, 2 * turn - 4))
     return jnp.where(even, of_even, of_odd)
 
 
 def more_down(home, which):
-    even = lax.rem(home, 2) == 0
+    even = low_bit(home) == 0
     lone = which == jnp.where(even, 1, 3)
     second = jnp.logical_or(which == 4, which == jnp.where(even, 2, 1))
-    return jnp.where(lone, lax.rem(lax.div(home, 2), 2), jnp.where(second, 1, 0))
+    return jnp.where(lone, low_bit(half(home)), jnp.where(second, 1, 0))
 
 
 def kernel(
@@ -285,16 +303,16 @@
     def gather_step(n):
         m = n - PER_Z
         middle = jnp.logical_and(n >= PER_Z, n < 35)
-        away = jnp.where(n < PER_Z, 0, jnp.where(middle, 1 + lax.div(m, 10), 4))
-        turn = jnp.where(n < PER_Z, n, jnp.where(middle, lax.div(lax.rem(m, 10), 2), n - 35))
-        rising = jnp.logical_and(middle, lax.rem(m, 2) == 0)
-        home = lax.rem(jnp.where(rising, z - away, z + away) + N_Z, N_Z)
+        away = jnp.where(n < PER_Z, 0, jnp.where(middle, 1 + tens(m), 4))
+        turn = jnp.where(n < PER_Z, n, jnp.where(middle, half(m - 10 * tens(m)), n - 35))
+        rising = jnp.logical_and(middle, low_bit(m) == 0)
+        home = round_z(jnp.where(rising, z - away, z + away))
         which = in_order(home, turn, False)
         block = PER_Z * home + which
         odd = more_down(home, which)
         mine = core_of(block) == core
         across = by_y(home, which)
-        mine_relay = jnp.logical_and(jnp.logical_and(mine, across), lax.div(which, 3) == my_y)
+        mine_relay = jnp.logical_and(jnp.logical_and(mine, across), jnp.where(which < 3, 0, 1) == my_y)
         mine_ring = jnp.logical_and(mine, jnp.logical_not(across))
         start = n < PER_Z
         falling = jnp.logical_and(middle, jnp.logical_not(rising))
@@ -309,28 +327,26 @@
         def _():
             gather_copy(place, True).wait_recv()
 
-        @pl.when(jnp.logical_and(mine_ring, send_up))
-        def _():
-            gather_copy(place, True).start()
-
-        @pl.when(jnp.logical_and(mine_ring, send_down))
-        def _():
-            gather_copy(place, False).start()
+            @pl.when(send_up)
+            def _():
+                gather_copy(place, True).start()
+
+            @pl.when(send_down)
+            def _():
+                gather_copy(place, False).start()
 
         @pl.when(mine_relay)
         def _():
             relay_copy(place, True).wait_recv()
 
-        @pl.when(jnp.logical_and(mine_relay, send_up))
-        def _():
-            relay_copy(place, True).start()
-
-        @pl.when(jnp.logical_and(mine_relay, send_down))
-        def _():
-            relay_copy(place, False).start()
-
-        @pl.when(mine_relay)
-        def _():
+            @pl.when(send_up)
+            def _():
+                relay_copy(place, True).start()
+
+            @pl.when(send_down)
+            def _():
+                relay_copy(place, False).start()
+
             for half_y in range(2):
                 relay_over(place, half_y).start()
 
@@ -440,14 +456,14 @@
     lax.fori_loop(0, 2 * MB, cotangent, 0)
 
     cosine, sine = cos_ref[...], sin_ref[...]
-    half = HEAD_SIZE // 2
+    middle_row = HEAD_SIZE // 2
 
     def rotate(value):
-        a, b = value[:half], value[half:]
+        a, b = value[:middle_row], value[middle_row:]
         return jnp.concatenate([a * cosine - b * sine, b * cosine + a * sine], axis=0)
 
     def rotate_back(value):
-        a, b = value[:half], value[half:]
+        a, b = value[:middle_row], value[middle_row:]
         return jnp.concatenate([a * cosine + b * sine, b * cosine - a * sine], axis=0)
 
     def attention(n, carry):
@@ -495,26 +511,39 @@
 
     lax.fori_loop(0, 8, attention, 0)
 
-    def sum_copy(place, going_up):
+    def part_rows(part):
+        return pl.ds(PART * part, PART)
+
+    def sum_copy(place, part, going_up, source):
         landing, arrived = (from_low, low_recv) if going_up else (from_high, high_recv)
         return pltpu.make_async_remote_copy(
-            src_ref=stage.at[place],
-            dst_ref=landing.at[place],
-            send_sem=sum_send.at[place],
-            recv_sem=arrived.at[place],
+            src_ref=source.at[place, part_rows(part)],
+            dst_ref=landing.at[place, part_rows(part)],
+            send_sem=sum_send.at[PARTS * place + part],
+            recv_sem=arrived.at[PARTS * place + part],
             device_id=(section, up if going_up else down),
             device_id_type=MESH,
         )
 
-    def give_copy(place, which):
+    def give_copy(place, part, which):
         return pltpu.make_async_remote_copy(
-            src_ref=stage.at[place],
-            dst_ref=given.at[my_y, place],
-            send_sem=give_send.at[place],
-            recv_sem=give_recv.at[LOCAL * my_y + place],
-            device_id=(partner, 4 * z + 2 * lax.div(which, 3) + core),
-            device_id_type=MESH,
-        )
+            src_ref=stage.at[place, part_rows(part)],
+            dst_ref=given.at[my_y, place, part_rows(part)],
+            send_sem=give_send.at[PARTS * place + part],
+            recv_sem=give_recv.at[PARTS * (LOCAL * my_y + place) + part],
+            device_id=(partner, 4 * z + 2 * jnp.where(which < 3, 0, 1) + core),
+            device_id_type=MESH,
+        )
+
+    def given_wait(place, part, source):
+        pltpu.make_async_remote_copy(
+            src_ref=given.at[source, place, part_rows(part)],
+            dst_ref=given.at[source, place, part_rows(part)],
+            send_sem=give_send.at[PARTS * place + part],
+            recv_sem=give_recv.at[PARTS * (LOCAL * source + place) + part],
+            device_id=(partner, dp),
+            device_id_type=MESH,
+        ).wait_recv()
 
     def keeper_of(which, quarter):
         inside = CHUNK * which + PIECE * quarter
@@ -547,32 +576,21 @@
             device_id_type=MESH,
         )
 
-    def relay_sum_copy(place, going_up):
-        landing, arrived = (from_low, low_recv) if going_up else (from_high, high_recv)
-        return pltpu.make_async_remote_copy(
-            src_ref=given.at[0, place],
-            dst_ref=landing.at[place],
-            send_sem=sum_send.at[place],
-            recv_sem=arrived.at[place],
-            device_id=(section, up if going_up else down),
-            device_id_type=MESH,
-        )
-
     def sum_step(n):
         m = n - PER_Z
         middle = jnp.logical_and(n >= PER_Z, n < 35)
         last = n >= 35
-        away = jnp.where(n < PER_Z, 4, jnp.where(middle, 3 - lax.div(m, 10), 0))
-        turn = jnp.where(n < PER_Z, n, jnp.where(middle, lax.div(lax.rem(m, 10), 2), n - 35))
-        falling = jnp.logical_and(middle, lax.rem(m, 2) == 1)
-        home = lax.rem(jnp.where(falling, z - away, z + away) + N_Z, N_Z)
+        away = jnp.where(n < PER_Z, 4, jnp.where(middle, 3 - tens(m), 0))
+        turn = jnp.where(n < PER_Z, n, jnp.where(middle, half(m - 10 * tens(m)), n - 35))
+        falling = jnp.logical_and(middle, low_bit(m) == 1)
+        home = round_z(jnp.where(falling, z - away, z + away))
         which = in_order(home, turn, True)
         block = PER_Z * home + which
         odd = more_down(home, which)
         mine = core_of(block) == core
         across = by_y(home, which)
         mine_give = jnp.logical_and(mine, across)
-        mine_relay = jnp.logical_and(mine_give, lax.div(which, 3) == my_y)
+        mine_relay = jnp.logical_and(mine_give, jnp.where(which < 3, 0, 1) == my_y)
         mine_ring = jnp.logical_and(mine, jnp.logical_not(across))
         rises = jnp.where(middle, jnp.logical_not(falling), odd == 0)
         has_low = jnp.logical_or(last, jnp.logical_and(rises, away < 4 - odd))
@@ -598,83 +616,90 @@
         def _():
             block_gradient(place)
             stage[place] = total[...].astype(BF16)
-            give_copy(place, which).start()
+            for part in range(PARTS):
+                give_copy(place, part, which).start()
 
     def reduce(n):
         place, which, mine_ring, _, mine_relay, has_low, has_high, go_up, go_down, last = sum_step(n)
 
+        def pass_on(part, buffer, keep):
+            rows = part_rows(part)
+            for going_up, has, landing in ((True, has_low, from_low), (False, has_high, from_high)):
+
+                @pl.when(has)
+                def _(going_up=going_up, landing=landing):
+                    sum_copy(place, part, going_up, buffer).wait_recv()
+                    total[rows, :] += landing[place, rows, :].astype(F32)
+
+            buffer[place, rows, :] = total[rows, :].astype(BF16)
+            for going_up, goes in ((True, go_up), (False, go_down)):
+
+                @pl.when(goes)
+                def _(going_up=going_up):
+                    sum_copy(place, part, going_up, buffer).start()
+
+            @pl.when(last)
+            def _():
+                for quarter in range(PART // PIECE * part, PART // PIECE * (part + 1)):
+                    keep(quarter)
+
+        def keep_ring(quarter):
+            final_copy(which, quarter).start()
+
+        def keep_relay(quarter):
+            keeper, _ = keeper_of(which, quarter)
+            here = low_bit(keeper) == core
+
+            @pl.when(here)
+            def _():
+                relay_final(which, quarter, True).start()
+
+            @pl.when(jnp.logical_not(here))
+            def _():
+                relay_final(which, quarter, False).start()
+
         @pl.when(mine_ring)
         def _():
             block_gradient(place)
+            for part in range(PARTS):
+                pass_on(part, stage, keep_ring)
 
         @pl.when(mine_relay)
         def _():
-            for source in range(2):
-                pltpu.make_async_remote_copy(
-                    src_ref=given.at[source, place],
-                    dst_ref=given.at[source, place],
-                    send_sem=give_send.at[place],
-                    recv_sem=give_recv.at[LOCAL * source + place],
-                    device_id=(partner, dp),
-                    device_id_type=MESH,
-                ).wait_recv()
-            total[...] = given[0, place].astype(F32) + given[1, place].astype(F32)
-
-        active = jnp.logical_or(mine_ring, mine_relay)
-
-        @pl.when(jnp.logical_and(active, has_low))
-        def _():
-            sum_copy(place, True).wait_recv()
-            total[...] += from_low[place].astype(F32)
-
-        @pl.when(jnp.logical_and(active, has_high))
-        def _():
-            sum_copy(place, False).wait_recv()
-            total[...] += from_high[place].astype(F32)
-
-        @pl.when(mine_ring)
-        def _():
-            stage[place] = total[...].astype(BF16)
-
-        @pl.when(mine_relay)
-        def _():
-            given[0, place] = total[...].astype(BF16)
-
-        for going_up, goes in ((True, go_up), (False, go_down)):
+            for part in range(PARTS):
+                rows = part_rows(part)
+                for source in range(2):
+                    given_wait(place, part, source)
+                total[rows, :] = given[0, place, rows, :].astype(F32) + given[1, place, rows, :].astype(F32)
+                pass_on(part, given.at[0], keep_relay)
+
+    def gather_sent(n):
+        place, mine_ring, mine_relay, send_up, send_down = gather_step(n)
+        for going_up, goes in ((True, send_up), (False, send_down)):
 
             @pl.when(jnp.logical_and(mine_ring, goes))
             def _(going_up=going_up):
-                sum_copy(place, going_up).start()
+                gather_copy(place, going_up).wait_send()
 
             @pl.when(jnp.logical_and(mine_relay, goes))
             def _(going_up=going_up):
-                relay_sum_copy(place, going_up).start()
-
-        @pl.when(jnp.logical_and(mine_ring, last))
-        def _():
-            for quarter in range(CHUNK // PIECE):
-                final_copy(which, quarter).start()
-
-        for quarter in range(CHUNK // PIECE):
-            keeper, _ = keeper_of(which, quarter)
-            here = lax.rem(keeper, 2) == core
-
-            @pl.when(jnp.logical_and(jnp.logical_and(mine_relay, last), here))
-            def _(quarter=quarter):
-                relay_final(which, quarter, True).start()
-
-            @pl.when(jnp.logical_and(jnp.logical_and(mine_relay, last), jnp.logical_not(here)))
-            def _(quarter=quarter):
-                relay_final(which, quarter, False).start()
+                relay_copy(place, going_up).wait_send()
+
+        @pl.when(mine_relay)
+        def _():
+            for half_y in range(2):
+                relay_over(place, half_y).wait_send()
 
     def lead(n, carry):
         give(n)
+        gather_sent(n)
         return carry
 
     def both(n, carry):
         @pl.when(n < 40)
         def _():
             give(n)
+            gather_sent(n)
 
         reduce(n - LEAD)
         return carry
@@ -697,41 +722,27 @@
             relay_piece(piece, False).wait_send()
 
     def drain(n, carry):
-        place, mine_ring, mine_relay, send_up, send_down = gather_step(n)
-        for going_up, goes in ((True, send_up), (False, send_down)):
-
-            @pl.when(jnp.logical_and(mine_ring, goes))
-            def _(going_up=going_up):
-                gather_copy(place, going_up).wait_send()
-
-            @pl.when(jnp.logical_and(mine_relay, goes))
-            def _(going_up=going_up):
-                relay_copy(place, going_up).wait_send()
-
-        @pl.when(mine_relay)
-        def _():
-            for half_y in range(2):
-                relay_over(place, half_y).wait_send()
-
         place, which, mine_ring, mine_give, mine_relay, _, _, _, _, last = sum_step(n)
-        active = jnp.logical_or(mine_ring, mine_relay)
-
-        @pl.when(jnp.logical_and(active, jnp.logical_not(last)))
-        def _():
-            sum_copy(place, True).wait_send()
 
         @pl.when(mine_give)
         def _():
-            give_copy(place, which).wait_send()
-
-        for quarter in range(CHUNK // PIECE):
-            keeper, _ = keeper_of(which, quarter)
-            away_core = lax.rem(keeper, 2) != core
-            sent_on = jnp.logical_or(mine_ring, jnp.logical_and(mine_relay, away_core))
-
-            @pl.when(jnp.logical_and(last, sent_on))
-            def _(quarter=quarter):
-                final_copy(which, quarter).wait_send()
+            for part in range(PARTS):
+                give_copy(place, part, which).wait_send()
+
+        @pl.when(jnp.logical_and(jnp.logical_or(mine_ring, mine_relay), jnp.logical_not(last)))
+        def _():
+            for part in range(PARTS):
+                sum_copy(place, part, True, stage).wait_send()
+
+        @pl.when(last)
+        def _():
+            for quarter in range(CHUNK // PIECE):
+                keeper, _ = keeper_of(which, quarter)
+                away_core = low_bit(keeper) != core
+
+                @pl.when(jnp.logical_or(mine_ring, jnp.logical_and(mine_relay, away_core)))
+                def _(quarter=quarter):
+                    final_copy(which, quarter).wait_send()
 
         return carry
 
@@ -815,11 +826,11 @@
             dma((MB,)),
             dma((MB,)),
             dma((MB,)),
-            dma((LOCAL,)),
-            dma((LOCAL,)),
-            dma((LOCAL,)),
-            dma((LOCAL,)),
-            dma((2 * LOCAL,)),
+            dma((PARTS * LOCAL,)),
+            dma((PARTS * LOCAL,)),
+            dma((PARTS * LOCAL,)),
+            dma((PARTS * LOCAL,)),
+            dma((2 * PARTS * LOCAL,)),
             dma((4 * PER_Z,)),
             dma((2 * PIECES,)),
         ],

time: 135 us -> 131 us (0.970)
  Pallas kernels: 130 us -> 126 us
    pallas_call x1, Pallas kernels: 130 us -> 126 us  [summed_gradient(): pl.pallas_call(kernel, out_shape=jax.ShapeDtypeStruct((SHARD, width), F32...]
where the time goes in v5:
time: 131 us
  Pallas kernels  126 us (96%)
  other arithmetic  2.78 us (2%)
  local copies, waits for them, and re-layouts  1.42 us (1%)
    pallas_call x1, Pallas kernels, summed_gradient(): pl.pallas_call(kernel, out_shape=jax.ShapeDtypeStruct((SHARD, width), F32...  126 us
    broadcast_in_dim x1, other arithmetic, shards(): return (renewed[None], first_new[None], second_new[None])  2.78 us

profile of v5, /device:TPU:6, one launch (start us, length us, event | category | flops | bytes accessed | tf_op | source)
XLA Modules:
  0.0 131.0 jit_solution(2464232484117748539)
XLA Ops:
  0.6 0.7 broadcast_in_dim.21
  1.3 0.1 broadcast_in_dim.22
  1.4 0.7 broadcast_in_dim.23.ids_ref
  2.0 0.0 copy-start
  2.0 0.0 copy-start.1
  2.0 0.0 copy-start.2
  2.0 126.1 %shard_map.103 = f32[80,2048]{1,0:T(8,128)} custom-call(bf16[80,2048]{1,0:T(8,128)(2,1)} %bitcast.25, bf16[4,192,2048]{2,1,0:T(8,128)(2,1)} %bitcast.23, bf16[4,192,2048]{2,1,0:T(8,128)(2,1)} %bitcast.24, s32[8,128]{1,0:T(8,128)} %broadcast_in_dim.23.ids_ref, f32[32,192]{1,0:T(8,128)} %constant.28.clone.cos_ref, f32[32,192]{1,0:T(8,128)} %constant.29.clone.sin_ref), custom_call_target="tpu_custom_call" | custom-call | tf_op jit(solution)/shard_map/pallas_call | solution.py:784
  128.2 0.0 copy-done
  128.2 0.0 copy-done.1
  128.2 0.0 copy-done.2
  128.2 2.8 %fusion.5 = (f32[1,80,2048]{2,1,0:T(8,128)}, bf16[1,80,2048]{2,1,0:T(8,128)(2,1)}, f32[1,80,2048]{2,1,0:T(8,128)}) fusion(f32[80,2048]{1,0:T(8,128)} %shard_map.103, f32[1,80,2048]{2,1,0:T(8,128)S(1)} %copy-done.1, f32[1,80,2048]{2,1,0:T(8,128)S(1)} %copy-done.2, bf16[1,80,2048]{2,1,0:T(8,128)(2,1)S(1)} %copy-done), kind=kLoop, calls=%fused_computation.9 | loop fusion | flops 2949120 | bytes 3932160 | tf_op jit(solution)/shard_map/broadcast_in_dim | solution.py:857
Async XLA Ops:
  2.0 126.1 %copy-start = (bf16[1,80,2048]{2,1,0:T(8,128)(2,1)S(1)}, bf16[1,80,2048]{2,1,0:T(8,128)(2,1)}, u32[]{:S(2)}) copy-start(bf16[1,80,2048]{2,1,0:T(8,128)(2,1)} %param.8) | copy-start | bytes 983044
  2.0 126.1 %copy-start.1 = (f32[1,80,2048]{2,1,0:T(8,128)S(1)}, f32[1,80,2048]{2,1,0:T(8,128)}, u32[]{:S(2)}) copy-start(f32[1,80,2048]{2,1,0:T(8,128)} %param.10) | copy-start | bytes 1966084
  2.0 126.1 %copy-start.2 = (f32[1,80,2048]{2,1,0:T(8,128)S(1)}, f32[1,80,2048]{2,1,0:T(8,128)}, u32[]{:S(2)}) copy-start(f32[1,80,2048]{2,1,0:T(8,128)} %param.9) | copy-start | bytes 1966084

commit v6 on v5

--- a/solution.py
+++ b/solution.py
@@ -22,7 +22,8 @@
 PER_Z = 5
 LOCAL = 20
 SHARD = 80
-LEAD = 12
+LEAD = 10
+LAG = 16
 STACK = 4
 PARTS = 1
 PART = CHUNK // PARTS
@@ -119,6 +120,7 @@
     shard,
     sent,
     back,
+    ids_own,
     ids_next,
     ids_prev,
     ids_one,
@@ -187,6 +189,9 @@
     for load in loads:
         load.start()
 
+    row_of = lax.broadcasted_iota(jnp.int32, (8, 128), 0)
+    ids_own[...] = jnp.where(row_of == 0, ids_ref[0, 0], ids_ref[0, 1])
+
     barrier = pltpu.get_barrier_semaphore()
     beyond = jnp.where(odd_section == 0, before, after)
     peers = [(section, sibling), (section, up), (section, down), (before_two, dp), (after_two, dp), (beyond, dp)]
@@ -198,7 +203,7 @@
 
     id_copies = [
         pltpu.make_async_remote_copy(
-            src_ref=ids_ref,
+            src_ref=ids_own,
             dst_ref=ids_next,
             send_sem=sem_ids_send.at[0],
             recv_sem=sem_ids_recv.at[0],
@@ -206,7 +211,7 @@
             device_id_type=MESH,
         ),
         pltpu.make_async_remote_copy(
-            src_ref=ids_ref,
+            src_ref=ids_own,
             dst_ref=ids_prev,
             send_sem=sem_ids_send.at[1],
             recv_sem=sem_ids_recv.at[1],
@@ -690,6 +695,31 @@
             for half_y in range(2):
                 relay_over(place, half_y).wait_send()
 
+    def drain(n, carry):
+        place, which, mine_ring, mine_give, mine_relay, _, _, _, _, last = sum_step(n)
+
+        @pl.when(mine_give)
+        def _():
+            for part in range(PARTS):
+                give_copy(place, part, which).wait_send()
+
+        @pl.when(jnp.logical_and(jnp.logical_or(mine_ring, mine_relay), jnp.logical_not(last)))
+        def _():
+            for part in range(PARTS):
+                sum_copy(place, part, True, stage).wait_send()
+
+        @pl.when(last)
+        def _():
+            for quarter in range(CHUNK // PIECE):
+                keeper, _ = keeper_of(which, quarter)
+                away_core = low_bit(keeper) != core
+
+                @pl.when(jnp.logical_or(mine_ring, jnp.logical_and(mine_relay, away_core)))
+                def _(quarter=quarter):
+                    final_copy(which, quarter).wait_send()
+
+        return carry
+
     def lead(n, carry):
         give(n)
         gather_sent(n)
@@ -702,6 +732,11 @@
             gather_sent(n)
 
         reduce(n - LEAD)
+
+        @pl.when(n >= LEAD + LAG)
+        def _():
+            drain(n - LEAD - LAG, 0)
+
         return carry
 
     lax.fori_loop(0, LEAD, lead, 0)
@@ -721,32 +756,7 @@
         def _(piece=piece):
             relay_piece(piece, False).wait_send()
 
-    def drain(n, carry):
-        place, which, mine_ring, mine_give, mine_relay, _, _, _, _, last = sum_step(n)
-
-        @pl.when(mine_give)
-        def _():
-            for part in range(PARTS):
-                give_copy(place, part, which).wait_send()
-
-        @pl.when(jnp.logical_and(jnp.logical_or(mine_ring, mine_relay), jnp.logical_not(last)))
-        def _():
-            for part in range(PARTS):
-                sum_copy(place, part, True, stage).wait_send()
-
-        @pl.when(last)
-        def _():
-            for quarter in range(CHUNK // PIECE):
-                keeper, _ = keeper_of(which, quarter)
-                away_core = low_bit(keeper) != core
-
-                @pl.when(jnp.logical_or(mine_ring, jnp.logical_and(mine_relay, away_core)))
-                def _(quarter=quarter):
-                    final_copy(which, quarter).wait_send()
-
-        return carry
-
-    lax.fori_loop(0, 40, drain, 0)
+    lax.fori_loop(40 - LAG, 40, drain, 0)
 
     def final_wait(piece, source):
         rows = pl.ds(PIECE * piece, PIECE)
@@ -777,19 +787,20 @@
     angles = frequency[:, None] * np.arange(SEQ, dtype=np.float64)[None, :]
     cosine = jnp.asarray(np.cos(angles), F32)
     sine = jnp.asarray(np.sin(angles), F32)
-    wide_ids = jnp.broadcast_to(ids.reshape(1, MB, 1), (4, MB, 128)).reshape(8, 128)
     dma = pltpu.SemaphoreType.DMA
     in_vmem = pl.BlockSpec(memory_space=pltpu.VMEM)
+    in_smem = pl.BlockSpec(memory_space=pltpu.SMEM)
     anywhere = pl.BlockSpec(memory_space=pl.ANY)
     return pl.pallas_call(
         kernel,
         out_shape=jax.ShapeDtypeStruct((SHARD, width), F32),
-        in_specs=[anywhere, anywhere, anywhere, in_vmem, in_vmem, in_vmem],
+        in_specs=[anywhere, anywhere, anywhere, in_smem, in_vmem, in_vmem],
         out_specs=in_vmem,
         scratch_shapes=[
             pltpu.VMEM((SHARD, width), BF16),
             pltpu.VMEM((LOG, SEQ, width), BF16),
             pltpu.VMEM((LOG, SEQ, width), BF16),
+            pltpu.VMEM((8, 128), jnp.int32),
             pltpu.VMEM((8, 128), jnp.int32),
             pltpu.VMEM((8, 128), jnp.int32),
             pltpu.SMEM((8, 128), jnp.int32),
@@ -837,7 +848,7 @@
         compiler_params=pltpu.CompilerParams(
             collective_id=0, has_side_effects=True, vmem_limit_bytes=60 * 1024 * 1024
         ),
-    )(params, sent, back, wide_ids, cosine, sine)
+    )(params, sent, back, ids.reshape(1, MB), cosine, sine)
 
 
 def apply_adam(weights, first_moment, second_moment, gradient):

time: 131 us -> 127 us (0.969)
  Pallas kernels: 126 us -> 123 us
  local copies, waits for them, and re-layouts: 1.42 us -> 0.01 us
    pallas_call x1, Pallas kernels: 126 us -> 123 us  [summed_gradient(): pl.pallas_call(kernel, out_shape=jax.ShapeDtypeStruct((SHARD, width), F32...]
    broadcast_in_dim x3 -> x0, local copies, waits for them, and re-layouts: 1.41 us -> none  [summed_gradient(): jnp.broadcast_to(ids.reshape(1, MB, 1), (4, MB, 128)).reshape(8, 128)]
where the time goes in v6:
time: 127 us; the launch traced here: 126 us
  Pallas kernels  123 us (97%)
  other arithmetic  2.78 us (2%)
    pallas_call x1, Pallas kernels, summed_gradient(): pl.pallas_call(kernel, out_shape=jax.ShapeDtypeStruct((SHARD, width), F32...  123 us
    broadcast_in_dim x1, other arithmetic, shards(): return (renewed[None], first_new[None], second_new[None])  2.78 us

profile of v6, /device:TPU:6, one launch (start us, length us, event | category | flops | bytes accessed | tf_op | source)
XLA Modules:
  0.0 126.2 jit_solution(10004576124833926319)
XLA Ops:
  0.6 0.0 copy-start
  0.6 0.0 copy-start.1
  0.7 0.0 copy-start.2
  0.7 122.7 %shard_map.103 = f32[80,2048]{1,0:T(8,128)} custom-call(bf16[80,2048]{1,0:T(8,128)(2,1)} %bitcast.25, bf16[4,192,2048]{2,1,0:T(8,128)(2,1)} %bitcast.23, bf16[4,192,2048]{2,1,0:T(8,128)(2,1)} %bitcast.24, s32[1,2]{1,0:T(1,128)} %bitcast.26, f32[32,192]{1,0:T(8,128)} %constant.28.clone.cos_ref, f32[32,192]{1,0:T(8,128)} %constant.29.clone.sin_ref), custom_call_target="tpu_custom_call" | custom-call | tf_op jit(solution)/shard_map/pallas_call | solution.py:794
  123.4 0.0 copy-done
  123.4 0.0 copy-done.1
  123.4 0.0 copy-done.2
  123.4 2.8 %fusion.5 = (f32[1,80,2048]{2,1,0:T(8,128)}, bf16[1,80,2048]{2,1,0:T(8,128)(2,1)}, f32[1,80,2048]{2,1,0:T(8,128)}) fusion(f32[80,2048]{1,0:T(8,128)} %shard_map.103, f32[1,80,2048]{2,1,0:T(8,128)S(1)} %copy-done.1, f32[1,80,2048]{2,1,0:T(8,128)S(1)} %copy-done.2, bf16[1,80,2048]{2,1,0:T(8,128)(2,1)S(1)} %copy-done), kind=kLoop, calls=%fused_computation.9 | loop fusion | flops 2949120 | bytes 3932160 | tf_op jit(solution)/shard_map/broadcast_in_dim | solution.py:868
Async XLA Ops:
  0.6 122.7 %copy-start = (bf16[1,80,2048]{2,1,0:T(8,128)(2,1)S(1)}, bf16[1,80,2048]{2,1,0:T(8,128)(2,1)}, u32[]{:S(2)}) copy-start(bf16[1,80,2048]{2,1,0:T(8,128)(2,1)} %param.8) | copy-start | bytes 983044
  0.6 122.7 %copy-start.1 = (f32[1,80,2048]{2,1,0:T(8,128)S(1)}, f32[1,80,2048]{2,1,0:T(8,128)}, u32[]{:S(2)}) copy-start(f32[1,80,2048]{2,1,0:T(8,128)} %param.10) | copy-start | bytes 1966084
  0.7 122.7 %copy-start.2 = (f32[1,80,2048]{2,1,0:T(8,128)S(1)}, f32[1,80,2048]{2,1,0:T(8,128)}, u32[]{:S(2)}) copy-start(f32[1,80,2048]{2,1,0:T(8,128)} %param.9) | copy-start | bytes 1966084

commit v7 on v6

--- a/solution.py
+++ b/solution.py
@@ -357,7 +357,7 @@
 
         return carry
 
-    lax.fori_loop(0, 3, gather, 0)
+    lax.fori_loop(0, 5, gather, 0)
 
     stays, leaves = odd_section, 1 - odd_section
     target_section = jnp.where(odd_section == 0, before_two, after_two)
@@ -413,7 +413,7 @@
         own_copies[m].start()
         own_locals[m].start()
 
-    lax.fori_loop(3, 40, gather, 0)
+    lax.fori_loop(5, 40, gather, 0)
 
     pass_copies = []
     for m in range(MB):
@@ -514,7 +514,7 @@
         lhs[batch, value_rows, :] = dvalue.astype(BF16)
         return carry
 
-    lax.fori_loop(0, 8, attention, 0)
+    lax.fori_loop(0, 8, attention, 0, unroll=2)
 
     def part_rows(part):
         return pl.ds(PART * part, PART)
@@ -846,7 +846,7 @@
             dma((2 * PIECES,)),
         ],
         compiler_params=pltpu.CompilerParams(
-            collective_id=0, has_side_effects=True, vmem_limit_bytes=60 * 1024 * 1024
+            collective_id=0, has_side_effects=True, vmem_limit_bytes=63 * 1024 * 1024
         ),
     )(params, sent, back, ids.reshape(1, MB), cosine, sine)
 

time: 127 us -> 125 us (0.984)
  the two profiles are of different devices: /device:TPU:6 before, /device:TPU:132 now
where the time goes in v7:
time: 125 us
  Pallas kernels  121 us (97%)
  other arithmetic  2.98 us (2%)
    pallas_call x1, Pallas kernels, summed_gradient(): pl.pallas_call(kernel, out_shape=jax.ShapeDtypeStruct((SHARD, width), F32...  121 us
    broadcast_in_dim x1, other arithmetic, shards(): return (renewed[None], first_new[None], second_new[None])  2.98 us

profile of v7, /device:TPU:132, one launch (start us, length us, event | category | flops | bytes accessed | tf_op | source)
XLA Modules:
  0.0 124.7 jit_solution(16715319585265565498)
XLA Ops:
  0.6 0.0 copy-start
  0.6 0.0 copy-start.1
  0.7 121.0 %shard_map.103 = f32[80,2048]{1,0:T(8,128)} custom-call(bf16[80,2048]{1,0:T(8,128)(2,1)} %bitcast.25, bf16[4,192,2048]{2,1,0:T(8,128)(2,1)} %bitcast.23, bf16[4,192,2048]{2,1,0:T(8,128)(2,1)} %bitcast.24, s32[1,2]{1,0:T(1,128)} %bitcast.26, f32[32,192]{1,0:T(8,128)} %constant.28.clone.cos_ref, f32[32,192]{1,0:T(8,128)} %constant.29.clone.sin_ref), custom_call_target="tpu_custom_call" | custom-call | tf_op jit(solution)/shard_map/pallas_call | solution.py:794
  121.7 0.0 copy-done
  121.7 0.0 copy-done.1
  121.7 3.0 %fusion.5 = (f32[1,80,2048]{2,1,0:T(8,128)}, bf16[1,80,2048]{2,1,0:T(8,128)(2,1)}, f32[1,80,2048]{2,1,0:T(8,128)}) fusion(f32[80,2048]{1,0:T(8,128)} %shard_map.103, f32[1,80,2048]{2,1,0:T(8,128)S(1)} %copy-done.1, f32[1,80,2048]{2,1,0:T(8,128)} %param.9, bf16[1,80,2048]{2,1,0:T(8,128)(2,1)S(1)} %copy-done), kind=kLoop, calls=%fused_computation.9 | loop fusion | flops 2949120 | bytes 3932160 | tf_op jit(solution)/shard_map/broadcast_in_dim | solution.py:868
Async XLA Ops:
  0.6 121.0 %copy-start = (bf16[1,80,2048]{2,1,0:T(8,128)(2,1)S(1)}, bf16[1,80,2048]{2,1,0:T(8,128)(2,1)}, u32[]{:S(2)}) copy-start(bf16[1,80,2048]{2,1,0:T(8,128)(2,1)} %param.8) | copy-start | bytes 983044
  0.6 121.0 %copy-start.1 = (f32[1,80,2048]{2,1,0:T(8,128)S(1)}, f32[1,80,2048]{2,1,0:T(8,128)}, u32[]{:S(2)}) copy-start(f32[1,80,2048]{2,1,0:T(8,128)} %param.10) | copy-start | bytes 1966084

commit v8 on v7

--- a/solution.py
+++ b/solution.py
@@ -439,8 +439,6 @@
 
         return carry
 
-    lax.fori_loop(0, 40, arrive, 0)
-
     for m in range(MB):
         own_locals[m].wait()
         own_copies[m].wait_recv()
@@ -451,14 +449,27 @@
         proj[batch] = nt(rows, acts[0, batch])
         return carry
 
-    lax.fori_loop(0, 2 * MB, project, 0)
-
     def cotangent(batch, carry):
         rows = weights[QKV_BLOCKS:].reshape(Q_ROWS, width)
         dctx[batch] = nt(rows, acts[1, batch]).astype(BF16)
         return carry
 
-    lax.fori_loop(0, 2 * MB, cotangent, 0)
+    def use(turn, carry):
+        output_side = low_bit(turn + jnp.where(z >= 4, 1, 0)) == 1
+
+        @pl.when(output_side)
+        def _():
+            lax.fori_loop(24, 40, arrive, 0)
+            lax.fori_loop(0, 2 * MB, cotangent, 0)
+
+        @pl.when(jnp.logical_not(output_side))
+        def _():
+            lax.fori_loop(0, 24, arrive, 0)
+            lax.fori_loop(0, 2 * MB, project, 0)
+
+        return carry
+
+    lax.fori_loop(0, 2, use, 0)
 
     cosine, sine = cos_ref[...], sin_ref[...]
     middle_row = HEAD_SIZE // 2

time: 125 us -> 125 us (level)
  the two profiles are of different devices: /device:TPU:132 before, /device:TPU:35 now
where the time goes in v8:
time: 125 us
  Pallas kernels  121 us (97%)
  other arithmetic  2.98 us (2%)
    pallas_call x1, Pallas kernels, summed_gradient(): pl.pallas_call(kernel, out_shape=jax.ShapeDtypeStruct((SHARD, width), F32...  121 us
    broadcast_in_dim x1, other arithmetic, shards(): return (renewed[None], first_new[None], second_new[None])  2.98 us

profile of v8, /device:TPU:35, one launch (start us, length us, event | category | flops | bytes accessed | tf_op | source)
XLA Modules:
  0.0 124.7 jit_solution(667651986912588221)
XLA Ops:
  0.6 0.0 copy-start
  0.6 0.0 copy-start.1
  0.7 121.0 %shard_map.103 = f32[80,2048]{1,0:T(8,128)} custom-call(bf16[80,2048]{1,0:T(8,128)(2,1)} %bitcast.25, bf16[4,192,2048]{2,1,0:T(8,128)(2,1)} %bitcast.23, bf16[4,192,2048]{2,1,0:T(8,128)(2,1)} %bitcast.24, s32[1,2]{1,0:T(1,128)} %bitcast.26, f32[32,192]{1,0:T(8,128)} %constant.28.clone.cos_ref, f32[32,192]{1,0:T(8,128)} %constant.29.clone.sin_ref), custom_call_target="tpu_custom_call" | custom-call | tf_op jit(solution)/shard_map/pallas_call | solution.py:805
  121.7 0.0 copy-done
  121.7 0.0 copy-done.1
  121.7 3.0 %fusion.5 = (f32[1,80,2048]{2,1,0:T(8,128)}, bf16[1,80,2048]{2,1,0:T(8,128)(2,1)}, f32[1,80,2048]{2,1,0:T(8,128)}) fusion(f32[80,2048]{1,0:T(8,128)} %shard_map.103, f32[1,80,2048]{2,1,0:T(8,128)S(1)} %copy-done.1, f32[1,80,2048]{2,1,0:T(8,128)} %param.9, bf16[1,80,2048]{2,1,0:T(8,128)(2,1)S(1)} %copy-done), kind=kLoop, calls=%fused_computation.9 | loop fusion | flops 2949120 | bytes 3932160 | tf_op jit(solution)/shard_map/broadcast_in_dim | solution.py:879
Async XLA Ops:
  0.6 121.0 %copy-start = (bf16[1,80,2048]{2,1,0:T(8,128)(2,1)S(1)}, bf16[1,80,2048]{2,1,0:T(8,128)(2,1)}, u32[]{:S(2)}) copy-start(bf16[1,80,2048]{2,1,0:T(8,128)(2,1)} %param.8) | copy-start | bytes 983044
  0.6 121.0 %copy-start.1 = (f32[1,80,2048]{2,1,0:T(8,128)S(1)}, f32[1,80,2048]{2,1,0:T(8,128)}, u32[]{:S(2)}) copy-start(f32[1,80,2048]{2,1,0:T(8,128)} %param.10) | copy-start | bytes 1966084
